TPU v7x, 512 devices: a whole 4x8x8 slice. The times are simulated.
512 devices in a mesh: pi: 2 (over y_hi), pj: 8 (over y_lo, core), pix: 32 (over z, x).
Axes of the slice: x: 4, y: 8 (y_hi: 2, y_lo: 4; y = y_hi * 4 + y_lo), z: 8, core: 2. Of those that a mesh axis runs over, the one named last changes fastest.
Arguments:
- images: bfloat16 [2, 64, 512, 128], P(None, ('pi', 'pj'), 'pix'), may hold values from -3.01 to 3.01, as said below
Outputs:
- coherence: bfloat16 [64, 64, 512, 128], P('pi', 'pj', 'pix')
Inputs may be any that keep to these rules, and one draw needn't show every extreme that they name: `images`: every complex entry has magnitude between 0.29 and 3.01.
All inputs are finite; a program needn't handle non-finite values.
Results may differ from a plain program's by a relative error of at most 0.001.
Values may be sent and summed in bfloat16 or wider, within the bound.
A program may use at most 64 MiB of HBM per device.

v0:
```python
import jax
import jax.numpy as jnp
from jax import lax
from jax.sharding import PartitionSpec as P

P_SIZE = 64


def with_halo(x, sides, width):
    for axis, dim in sides:
        size, length = (lax.axis_size(axis), x.shape[dim])
        up = [(i, (i + 1) % size) for i in range(size - 1)]
        down = [(j, i) for i, j in up]
        last = lax.slice_in_dim(x, length - width, length, axis=dim)
        first = lax.slice_in_dim(x, 0, width, axis=dim)
        before = lax.ppermute(last, axis, up)
        after = lax.ppermute(first, axis, down)
        x = jnp.concatenate([before, x, after], axis=dim)
    return x


def sum_columns(values):
    pad_width = [(0, 0)] * (values.ndim - 1) + [(3, 3)]
    padded = jnp.pad(values, pad_width)
    length = values.shape[-1]
    axis_last = values.ndim - 1
    total = lax.slice_in_dim(padded, 0, length, axis=axis_last)
    for offset in range(1, 7):
        total = total + lax.slice_in_dim(padded, offset, offset + length, axis=axis_last)
    return total


def sum_rows_inner(values, axis):
    length = values.shape[axis] - 6
    total = lax.slice_in_dim(values, 0, length, axis=axis)
    for offset in range(1, 7):
        total = total + lax.slice_in_dim(values, offset, offset + length, axis=axis)
    return total


def pair_terms(first_block, second_block):
    first_real = first_block[0].astype(jnp.float32)
    first_imag = first_block[1].astype(jnp.float32)
    second_real = second_block[0].astype(jnp.float32)
    second_imag = second_block[1].astype(jnp.float32)
    height = first_real.shape[1]
    width = first_real.shape[2]
    cross_real = first_real[:, None] * second_real[None] + first_imag[:, None] * second_imag[None]
    cross_imag = first_imag[:, None] * second_real[None] - first_real[:, None] * second_imag[None]
    power_first = first_real * first_real + first_imag * first_imag
    power_second = second_real * second_real + second_imag * second_imag
    return jnp.concatenate(
        [
            cross_real.reshape(-1, height, width),
            cross_imag.reshape(-1, height, width),
            power_first,
            power_second,
        ],
        axis=0,
    )


def finish(windowed, first_count, second_count):
    pairs = first_count * second_count
    height = windowed.shape[1]
    width = windowed.shape[2]
    sum_real = windowed[:pairs].reshape(first_count, second_count, height, width)
    sum_imag = windowed[pairs : 2 * pairs].reshape(first_count, second_count, height, width)
    power_first = windowed[2 * pairs : 2 * pairs + first_count]
    power_second = windowed[2 * pairs + first_count :]
    magnitude = jnp.sqrt(sum_real * sum_real + sum_imag * sum_imag) * lax.rsqrt(
        power_first[:, None] * power_second[None]
    )
    return magnitude.astype(jnp.bfloat16)


def per_device(images):
    first_index = lax.axis_index("pi")
    second_index = lax.axis_index("pj")
    first_count = P_SIZE // lax.axis_size("pi")
    second_count = P_SIZE // lax.axis_size("pj")
    everything = lax.all_gather(images, ("pi", "pj"), axis=1, tiled=True)
    first_block = lax.dynamic_slice_in_dim(everything, first_index * first_count, first_count, 1)
    second_block = lax.dynamic_slice_in_dim(
        everything, second_index * second_count, second_count, 1
    )
    joined = jnp.concatenate([first_block, second_block], axis=1)
    extended = with_halo(joined, (("pix", 2),), 3)
    terms = sum_columns(pair_terms(extended[:, :first_count], extended[:, first_count:]))
    windowed = sum_rows_inner(terms, 1)
    return finish(windowed, first_count, second_count)


def solution(mesh):
    placed = (P(None, ("pi", "pj"), "pix", None),)
    return jax.shard_map(
        per_device,
        mesh=mesh,
        in_specs=placed,
        out_specs=P("pi", "pj", "pix", None),
        check_vma=False,
    )
```

profile of v0, /device:TPU:198, one launch (start us, length us, event | category | flops | bytes accessed | tf_op | source)
XLA Modules:
  0.0 92.5 jit_solution(9567023301646119792)
XLA Ops:
  0.0 19.2 %all_gather.3 = bf16[2,64,16,128]{3,2,1,0:T(8,128)(2,1)S(1)} all-gather(bf16[2,4,16,128]{3,2,1,0:T(8,128)(2,1)} %param.1), channel_id=1, replica_groups=mesh['pi'=2,'pj'=8,'pix'=32] {'pi','pj'}, dimensions={1}, use_global_device_ids=true | all-gather | bytes 557056 | tf_op jit(solution)/shard_map/all_gather | solution.py:82
  19.3 0.1 pad_maximum_fusion.3
  19.4 5.4 %collective-permute-start = (bf16[2,40,3,128]{3,2,1,0:T(4,128)(2,1)S(1)}, bf16[2,40,3,128]{3,2,1,0:T(4,128)(2,1)S(1)}, u32[]{:S(2)}, u32[]{:S(2)}) collective-permute-start(bf16[2,40,3,128]{3,2,1,0:T(4,128)(2,1)S(1)} %get-tuple-element.15), channel_id=1, source_target_pairs={{0,1},{1,2},{2,3},{3,4},{4,5},{5,6},{6,7},{7,8},{8,9},{9,10},{10,1... | collective-permute-start | bytes 184328 | tf_op jit(solution)/shard_map/ppermute | solution.py:16
  24.8 1.9 %collective-permute-start.1 = (bf16[2,40,3,128]{3,2,1,0:T(4,128)(2,1)S(1)}, bf16[2,40,3,128]{3,2,1,0:T(4,128)(2,1)S(1)}, u32[]{:S(2)}, u32[]{:S(2)}) collective-permute-start(bf16[2,40,3,128]{3,2,1,0:T(4,128)(2,1)S(1)} %get-tuple-element.16), channel_id=1, source_target_pairs={{1,0},{2,1},{3,2},{4,3},{5,4},{6,5},{7,6},{8,7},{9,8},{10,9},{11,1... | collective-permute-start | bytes 184328 | tf_op jit(solution)/shard_map/ppermute | solution.py:17
  26.7 0.3 collective-permute-done
  27.0 7.5 %collective-permute-done.1 = bf16[2,40,3,128]{3,2,1,0:T(4,128)(2,1)S(1)} collective-permute-done((bf16[2,40,3,128]{3,2,1,0:T(4,128)(2,1)S(1)}, bf16[2,40,3,128]{3,2,1,0:T(4,128)(2,1)S(1)}, u32[]{:S(2)}, u32[]{:S(2)}) %collective-permute-start.1) | collective-permute-done | bytes 61472 | tf_op jit(solution)/shard_map/ppermute | solution.py:17
  34.4 0.3 pad_maximum_fusion.1
  34.7 0.1 multiply_add_fusion.1
  34.8 0.1 fusion.9
  34.9 0.7 fusion.11
  35.5 2.6 %multiply_add_fusion = (f32[32,8,22,128]{3,2,1,0:T(8,128)S(1)}, f32[32,8,22,128]{3,2,1,0:T(8,128)}) fusion(f32[8,22,128]{2,1,0:T(8,128)S(1)} %get-tuple-element.7, f32[32,22,128]{2,1,0:T(8,128)S(1)} %get-tuple-element.12, f32[8,22,128]{2,1,0:T(8,128)S(1)} %get-tuple-element.13, f32[32,22,128]{2,1,0:T(8,128)S(1)} %get-tuple-element.11), kind=kLoop, calls=%fused_computation.20 | loop fusion | flops 4325376 | bytes 6668288 | tf_op jit(solution)/shard_map/add | solution.py:48
  38.2 7.5 %pad_maximum_fusion = f32[552,22,128]{2,1,0:T(8,128)} fusion(f32[8,22,128]{2,1,0:T(8,128)} %fusion.11, f32[32,22,128]{2,1,0:T(8,128)S(1)} %multiply_add_fusion.1, f32[256,22,128]{2,1,0:T(8,128)} %bitcast.24, f32[256,22,128]{2,1,0:T(8,128)S(1)} %bitcast.23), kind=kLoop, calls=%fused_computation.12 | loop fusion | flops 4663296 | bytes 12435456 | tf_op jit(solution)/shard_map/concatenate | solution.py:52
  45.7 27.5 %fusion.5 = f32[552,22,128]{2,1,0:T(8,128)} fusion(f32[552,22,128]{2,1,0:T(8,128)} %pad_maximum_fusion), kind=kLoop, calls=%fused_computation.11 | loop fusion | flops 9326592 | bytes 12435456 | tf_op jit(solution)/shard_map/add | solution.py:29
  73.2 17.3 %slice_add_fusion = f32[552,16,128]{2,1,0:T(8,128)S(1)} fusion(f32[552,22,128]{2,1,0:T(8,128)} %fusion.5), kind=kLoop, calls=%fused_computation.13 | loop fusion | flops 6782976 | bytes 36175872 | tf_op jit(solution)/shard_map/add | solution.py:37
  90.5 0.7 fusion.7
  91.2 1.3 %multiply_convert_fusion = bf16[32,8,16,128]{3,2,1,0:T(8,128)(2,1)} fusion(f32[32,8,16,128]{3,2,1,0:T(8,128)S(1)} %bitcast.25, f32[8,16,128]{2,1,0:T(8,128)S(1)} %slice.111, f32[32,16,128]{2,1,0:T(8,128)S(1)} %slice.110), kind=kLoop, calls=%fused_computation.25 | loop fusion | flops 1572864 | bytes 3473408 | tf_op jit(solution)/shard_map/convert_element_type | solution.py:74
  (5 shorter events, 0.1 us)
Async XLA Ops:
  19.4 7.6 %collective-permute-start = (bf16[2,40,3,128]{3,2,1,0:T(4,128)(2,1)S(1)}, bf16[2,40,3,128]{3,2,1,0:T(4,128)(2,1)S(1)}, u32[]{:S(2)}, u32[]{:S(2)}) collective-permute-start(bf16[2,40,3,128]{3,2,1,0:T(4,128)(2,1)S(1)} %get-tuple-element.15), channel_id=1, source_target_pairs={{0,1},{1,2},{2,3},{3,4},{4,5},{5,6},{6,7},{7,8},{8,9},{9,10},{10,1... | collective-permute-start | bytes 184328 | tf_op jit(solution)/shard_map/ppermute | solution.py:16
  24.8 9.7 %collective-permute-start.1 = (bf16[2,40,3,128]{3,2,1,0:T(4,128)(2,1)S(1)}, bf16[2,40,3,128]{3,2,1,0:T(4,128)(2,1)S(1)}, u32[]{:S(2)}, u32[]{:S(2)}) collective-permute-start(bf16[2,40,3,128]{3,2,1,0:T(4,128)(2,1)S(1)} %get-tuple-element.16), channel_id=1, source_target_pairs={{1,0},{2,1},{3,2},{4,3},{5,4},{6,5},{7,6},{8,7},{9,8},{10,9},{11,1... | collective-permute-start | bytes 184328 | tf_op jit(solution)/shard_map/ppermute | solution.py:17
where the time goes:
time: 92.6 us; the launch traced here: 92.5 us
  other arithmetic  58 us (63%)
  blocking collectives  19.2 us (21%)
  waiting for transfers between devices  7.73 us (8%)
  starting transfers between devices  7.33 us (8%)
    add x1, other arithmetic, sum_columns(): total + lax.slice_in_dim(padded, offset, offset + length, axis=axis_last)  27.5 us
    all_gather x1, blocking collectives, per_device(): everything = lax.all_gather(images, ('pi', 'pj'), axis=1, tiled=True)  19.2 us
    add x1, other arithmetic, sum_rows_inner(): total = total + lax.slice_in_dim(values, offset, offset + length, axis=axis)  17.3 us
    concatenate x1, other arithmetic, pair_terms(): jnp.concatenate([cross_real.reshape(-1, height, width), cross_imag.reshap...  7.5 us
    ppermute x1, waiting for transfers between devices, with_halo(): after = lax.ppermute(first, axis, down)  7.46 us
    ppermute x1, starting transfers between devices, with_halo(): before = lax.ppermute(last, axis, up)  5.41 us
    add x1, other arithmetic, pair_terms(): first_real[:, None] * second_real[None]  2.65 us
    ppermute x1, starting transfers between devices, with_halo(): after = lax.ppermute(first, axis, down)  1.92 us
  transfers between devices with their start and end apart: 2, of which 2 were waited for; matrix products, arithmetic and copies ran while one was open for 0% of the time, Pallas kernels for 0%

commit v1 on v0

v1 whole, which is shorter than its diff:
```python
import jax
import jax.numpy as jnp
from jax import lax
from jax.experimental import pallas as pl
from jax.experimental.pallas import tpu as pltpu
from jax.sharding import PartitionSpec as P

BF = jnp.bfloat16
F32 = jnp.float32
MESH = pl.DeviceIdType.MESH
WINDOW = 22
COLS = 128
MATES = 8
UNROLL = 4


def table_row(group, part, row):
    return ((group * 2 + part) * WINDOW + row) * 8


def sum_seven(x):
    pairs = {j: x[j] + x[j + 1] for j in range(1, 20, 2)}
    out = []
    for i in range(0, 16, 2):
        middle = pairs[i + 1] + pairs[i + 3] + pairs[i + 5]
        out.append(x[i] + middle)
        out.append(middle + x[i + 7])
    return out


def sum_columns(rows, band):
    x = jnp.concatenate(rows, axis=0)
    high = x.astype(BF)
    low = (x - high.astype(F32)).astype(BF)
    return jnp.dot(jnp.concatenate([high, low], axis=1), band, preferred_element_type=F32)


def band_matrix():
    r = lax.broadcasted_iota(jnp.int32, (COLS, COLS), 0)
    c = lax.broadcasted_iota(jnp.int32, (COLS, COLS), 1)
    band = jnp.where(jnp.abs(r - c) <= 3, 1.0, 0.0).astype(BF)
    return jnp.concatenate([band, band], axis=0)


def spread_image(block, table, group, half):
    for part in range(2):
        for p in range(4):
            rows = block[part, p].astype(F32)
            for j in range(2):
                start = table_row(group, part, 3 + 8 * j) + half * 4 + p
                table[pl.ds(start, 8, stride=8), :] = rows[8 * j : 8 * j + 8]


def spread_halo(halo, table, group, half, pix, last):
    for edge in range(2):
        outside = (pix == 0) if edge == 0 else (pix == last)
        rows = jnp.where(outside, 0.0, halo[edge].astype(F32))
        for part in range(2):
            for k in range(3):
                start = table_row(group, part, (0 if edge == 0 else 19) + k) + half * 4
                table[pl.ds(start, 4), :] = rows[(part * 3 + k) * 4 : (part * 3 + k) * 4 + 4]


def inverse_root_power(table, scale, group, band):
    power = []
    for k in range(WINDOW):
        a = table[pl.ds(table_row(group, 0, k), 8), :]
        b = table[pl.ds(table_row(group, 1, k), 8), :]
        power.append(a * a + b * b)
    scale[pl.ds(group * 128, 128), :] = lax.rsqrt(sum_columns(sum_seven(power), band))


def coherence_of(m, second, table, scale, stage, out, band):
    group, s = m // 8, m % 8
    real, imag = [], []
    for k in range(WINDOW):
        a = jnp.broadcast_to(table[pl.ds(table_row(group, 0, k) + s, 1), :], (8, COLS))
        b = jnp.broadcast_to(table[pl.ds(table_row(group, 1, k) + s, 1), :], (8, COLS))
        c = table[pl.ds(table_row(second, 0, k), 8), :]
        d = table[pl.ds(table_row(second, 1, k), 8), :]
        real.append(a * c + b * d)
        imag.append(b * c - a * d)
    w = sum_columns(sum_seven(real) + sum_seven(imag), band)
    for r in range(16):
        x = w[r * 8 : r * 8 + 8]
        y = w[128 + r * 8 : 128 + r * 8 + 8]
        q = x * x + y * y
        first = jnp.broadcast_to(scale[pl.ds(group * 128 + r * 8 + s, 1), :], (8, COLS))
        other = scale[pl.ds(second * 128 + r * 8, 8), :]
        value = (q * lax.rsqrt(jnp.maximum(q, 1e-36))) * (first * other)
        stage[pl.ds(r, 8, stride=16), :] = value
    for n in range(8):
        out[m, n] = stage[pl.ds(n * 16, 16), :].astype(BF)


def kernel(images, out, blocks, halos, edges, edge_rows, table, scale, stage,
           pix_send, pix_recv, block_send, block_recv, halo_send, halo_recv):
    pi, pj, pix = lax.axis_index("pi"), lax.axis_index("pj"), lax.axis_index("pix")
    strips = lax.axis_size("pix")
    up, down = lax.rem(pix + strips - 1, strips), lax.rem(pix + 1, strips)
    far = (pj // 4) != pi
    barrier = pltpu.get_barrier_semaphore()
    for strip in (up, down):
        pl.semaphore_signal(barrier, inc=1, device_id={"pix": strip}, device_id_type=MESH)
    for off in range(1, MATES):
        pl.semaphore_signal(barrier, inc=1, device_id={"pj": lax.rem(pj + off, MATES)}, device_id_type=MESH)

    @pl.when(far)
    def _():
        for core in range(2):
            pl.semaphore_signal(
                barrier, inc=1, device_id={"pi": 1 - pi, "pj": 2 * lax.rem(pj, 4) + core}, device_id_type=MESH
            )

    spread_image(images, table, pj // 2, lax.rem(pj, 2))
    blocks[pj] = images[...]
    edge_rows[...] = jnp.zeros_like(edge_rows)
    for edge in range(2):
        for part in range(2):
            for k in range(3):
                start = table_row(pj // 2, part, (3 if edge == 0 else 16) + k) + lax.rem(pj, 2) * 4
                edge_rows[edge, pl.ds((part * 3 + k) * 4, 4), :] = table[pl.ds(start, 4), :]
    edges[...] = edge_rows[...].astype(BF)
    band = band_matrix()

    pl.semaphore_wait(barrier, 2 + (MATES - 1) + 1)

    to_strips = []
    for edge, strip in ((0, up), (1, down)):
        copy = pltpu.make_async_remote_copy(
            src_ref=edges.at[edge], dst_ref=halos.at[pj, 1 - edge], send_sem=pix_send.at[edge],
            recv_sem=pix_recv.at[1 - edge], device_id={"pix": strip}, device_id_type=MESH)
        copy.start()
        to_strips.append(copy)

    far_target = {"pi": 1 - pi, "pj": 4 * pi + pj // 2}

    def sends(source, place, send_sem, recv_sem):
        copies = []
        copies.append(pltpu.make_async_remote_copy(
            src_ref=source, dst_ref=place.at[MATES + lax.rem(pj, 2)], send_sem=send_sem.at[0],
            recv_sem=recv_sem.at[MATES + lax.rem(pj, 2)], device_id=far_target, device_id_type=MESH))
        for off in range(1, MATES):
            copies.append(pltpu.make_async_remote_copy(
                src_ref=source, dst_ref=place.at[pj], send_sem=send_sem.at[off],
                recv_sem=recv_sem.at[pj], device_id={"pj": lax.rem(pj + off, MATES)}, device_id_type=MESH))
        for copy in copies:
            copy.start()
        return copies

    block_copies = sends(images, blocks, block_send, block_recv)
    for copy in to_strips:
        copy.wait()
    halo_copies = sends(halos.at[pj], halos, halo_send, halo_recv)

    def arrived(slot):
        def wait(place, sem):
            pltpu.make_async_remote_copy(
                src_ref=place.at[slot], dst_ref=place.at[slot], send_sem=sem.at[slot], recv_sem=sem.at[slot],
                device_id={"pj": lax.rem(pj + 1, MATES)}, device_id_type=MESH).wait_recv()
        wait(blocks, block_recv)
        wait(halos, halo_recv)

    def take(group):
        def one(half, _):
            slot = group * 2 + half

            @pl.when(slot != pj)
            def _():
                arrived(slot)

            spread_image(blocks.at[slot], table, group, half)
            spread_halo(halos.at[slot], table, group, half, pix, strips - 1)
            return 0

        lax.fori_loop(0, 2, one, 0)
        inverse_root_power(table, scale, group, band)

    @pl.when(far)
    def _():
        take(MATES // 2)

    second = jnp.where(far, MATES // 2, lax.rem(pj, 4))
    start = jnp.where(far, pj // 2, lax.rem(pj, 4))

    def step(i, _):
        group = lax.rem(start + i, 4)
        take(group)

        def one(s, _):
            coherence_of(group * 8 + s, second, table, scale, stage, out, band)
            return 0

        lax.fori_loop(0, 8, one, 0, unroll=UNROLL)
        return 0

    lax.fori_loop(0, 4, step, 0)
    for copy in block_copies + halo_copies:
        copy.wait_send()


def per_device(images):
    return pl.pallas_call(
        kernel,
        out_shape=pltpu.VMEM((32, 8, 16, COLS), BF),
        in_specs=[pl.BlockSpec(memory_space=pltpu.VMEM)],
        out_specs=pl.BlockSpec(memory_space=pltpu.VMEM),
        scratch_shapes=[
            pltpu.VMEM((MATES + 2, 2, 4, 16, COLS), BF),
            pltpu.VMEM((MATES + 2, 2, 32, COLS), BF),
            pltpu.VMEM((2, 32, COLS), BF),
            pltpu.VMEM((2, 32, COLS), F32),
            pltpu.VMEM((5 * 2 * WINDOW * 8, COLS), F32),
            pltpu.VMEM((5 * 128, COLS), F32),
            pltpu.VMEM((128, COLS), F32),
            pltpu.SemaphoreType.DMA((2,)),
            pltpu.SemaphoreType.DMA((2,)),
            pltpu.SemaphoreType.DMA((MATES,)),
            pltpu.SemaphoreType.DMA((MATES + 2,)),
            pltpu.SemaphoreType.DMA((MATES,)),
            pltpu.SemaphoreType.DMA((MATES + 2,)),
        ],
        compiler_params=pltpu.CompilerParams(
            collective_id=0, has_side_effects=True, vmem_limit_bytes=24 << 20
        ),
        name="coherence",
    )(images)


def solution(mesh):
    return jax.shard_map(
        per_device,
        mesh=mesh,
        in_specs=(P(None, ("pi", "pj"), "pix", None),),
        out_specs=P("pi", "pj", "pix", None),
        check_vma=False,
    )
```

time: 92.6 us -> 30.9 us (0.33)
  the two profiles are of different devices: /device:TPU:198 before, /device:TPU:24 now
where the time goes in v1:
time: 30.9 us; the launch traced here: 30.8 us
  Pallas kernels  29 us (94%)
  local copies, waits for them, and re-layouts  1.73 us (6%)
    pallas_call x1, Pallas kernels, per_device(): pl.pallas_call(kernel, out_shape=pltpu.VMEM((32, 8, 16, COLS), BF), in_sp...  29 us
    unnamed x3, local copies, waits for them, and re-layouts  1.73 us

profile of v1, /device:TPU:24, one launch (start us, length us, event | category | flops | bytes accessed | tf_op | source)
XLA Modules:
  0.0 30.8 jit_solution(16060305945915676545)
XLA Ops:
  0.0 0.0 copy-start
  0.0 0.8 %copy-done = bf16[2,4,16,128]{3,2,1,0:T(8,128)(2,1)S(1)} copy-done((bf16[2,4,16,128]{3,2,1,0:T(8,128)(2,1)S(1)}, bf16[2,4,16,128]{3,2,1,0:T(8,128)(2,1)}, u32[]{:S(2)}) %copy-start) | copy-done | bytes 32792
  0.8 29.0 %coherence.1 = bf16[32,8,16,128]{3,2,1,0:T(8,128)(2,1)S(1)} custom-call(bf16[2,4,16,128]{3,2,1,0:T(8,128)(2,1)S(1)} %copy-done), custom_call_target="tpu_custom_call" | custom-call | tf_op jit(solution)/shard_map/coherence/pallas_call | solution.py:203
  29.8 1.0 %copy.3 = bf16[32,8,16,128]{3,2,1,0:T(8,128)(2,1)} copy(bf16[32,8,16,128]{3,2,1,0:T(8,128)(2,1)S(1)} %coherence.1) | data formatting | bytes 2097152
Async XLA Ops:
  0.0 0.8 %copy-start = (bf16[2,4,16,128]{3,2,1,0:T(8,128)(2,1)S(1)}, bf16[2,4,16,128]{3,2,1,0:T(8,128)(2,1)}, u32[]{:S(2)}) copy-start(bf16[2,4,16,128]{3,2,1,0:T(8,128)(2,1)} %images.1) | copy-start | bytes 98308

commit v2 on v1

v2 whole, which is shorter than its diff:
```python
import jax
import jax.numpy as jnp
from jax import lax
from jax.experimental import pallas as pl
from jax.experimental.pallas import tpu as pltpu
from jax.sharding import PartitionSpec as P

BF = jnp.bfloat16
F32 = jnp.float32
MESH = pl.DeviceIdType.MESH
WINDOW = 22
COLS = 128
MATES = 8
EDGE = 24
UNROLL = 4


def table_row(group, part, row):
    return ((group * 2 + part) * WINDOW + row) * 8


def sum_seven(x):
    pairs = {j: x[j] + x[j + 1] for j in range(1, 20, 2)}
    out = []
    for i in range(0, 16, 2):
        middle = pairs[i + 1] + pairs[i + 3] + pairs[i + 5]
        out.append(x[i] + middle)
        out.append(middle + x[i + 7])
    return out


def sum_columns(rows, band):
    x = jnp.concatenate(rows, axis=0)
    high = x.astype(BF)
    low = (x - high.astype(F32)).astype(BF)
    return jnp.dot(jnp.concatenate([high, low], axis=1), band, preferred_element_type=F32)


def band_matrix():
    r = lax.broadcasted_iota(jnp.int32, (COLS, COLS), 0)
    c = lax.broadcasted_iota(jnp.int32, (COLS, COLS), 1)
    band = jnp.where(jnp.abs(r - c) <= 3, 1.0, 0.0).astype(BF)
    return jnp.concatenate([band, band], axis=0)


def spread_image(block, table, group, half):
    for part in range(2):
        for p in range(4):
            rows = block[part, p].astype(F32)
            for j in range(2):
                start = table_row(group, part, 3 + 8 * j) + half * 4 + p
                table[pl.ds(start, 8, stride=8), :] = rows[8 * j : 8 * j + 8]


def spread_halo(halo, table, group, half):
    rows = halo[...].astype(F32)
    for edge in range(2):
        for part in range(2):
            for k in range(3):
                start = table_row(group, part, (0 if edge == 0 else 19) + k) + half * 4
                first = EDGE * edge + (part * 3 + k) * 4
                table[pl.ds(start, 4), :] = rows[first : first + 4]


def inverse_root_power(table, scale, group, band):
    power = []
    for k in range(WINDOW):
        a = table[pl.ds(table_row(group, 0, k), 8), :]
        b = table[pl.ds(table_row(group, 1, k), 8), :]
        power.append(a * a + b * b)
    scale[pl.ds(group * 128, 128), :] = lax.rsqrt(sum_columns(sum_seven(power), band))


def coherence_of(m, second, table, scale, stage, out, band):
    group, s = m // 8, m % 8
    real, imag = [], []
    for k in range(WINDOW):
        a = jnp.broadcast_to(table[pl.ds(table_row(group, 0, k) + s, 1), :], (8, COLS))
        b = jnp.broadcast_to(table[pl.ds(table_row(group, 1, k) + s, 1), :], (8, COLS))
        c = table[pl.ds(table_row(second, 0, k), 8), :]
        d = table[pl.ds(table_row(second, 1, k), 8), :]
        real.append(a * c + b * d)
        imag.append(b * c - a * d)
    w = sum_columns(sum_seven(real) + sum_seven(imag), band)
    for r in range(16):
        x = w[r * 8 : r * 8 + 8]
        y = w[128 + r * 8 : 128 + r * 8 + 8]
        q = x * x + y * y
        first = jnp.broadcast_to(scale[pl.ds(group * 128 + r * 8 + s, 1), :], (8, COLS))
        other = scale[pl.ds(second * 128 + r * 8, 8), :]
        value = (q * lax.rsqrt(jnp.maximum(q, 1e-36))) * (first * other)
        stage[pl.ds(r, 8, stride=16), :] = value
    for n in range(8):
        out[m, n] = stage[pl.ds(n * 16, 16), :].astype(BF)


def kernel(images, out, own, blocks, halos, edges, from_strips, edge_rows, table, scale, stage,
           own_sem, pix_send, pix_recv, block_send, block_recv, pass_send, halo_send, halo_recv):
    pi, pj, pix = lax.axis_index("pi"), lax.axis_index("pj"), lax.axis_index("pix")
    last = lax.axis_size("pix") - 1
    chip, core = pj // 2, lax.rem(pj, 2)
    far = (pj // 4) != pi
    not_first, not_last = pix > 0, pix < last

    def mate(chips, cores=0):
        return {"pj": 2 * lax.rem(chip + chips, 4) + lax.rem(core + cores, 2)}

    mates = [mate(3, 0), mate(3, 1), mate(2, 0), mate(2, 1), mate(1, 0), mate(1, 1), mate(0, 1)]
    far_target = {"pi": 1 - pi, "pj": 4 * pi + chip}

    fetch = pltpu.make_async_copy(images, own, own_sem)
    fetch.start()
    barrier = pltpu.get_barrier_semaphore()

    def greet(device):
        pl.semaphore_signal(barrier, inc=1, device_id=device, device_id_type=MESH)

    @pl.when(far)
    def _():
        for c in range(2):
            greet({"pi": 1 - pi, "pj": 2 * lax.rem(pj, 4) + c})

    for device in mates:
        greet(device)

    @pl.when(not_first)
    def _():
        greet({"pix": pix - 1})

    @pl.when(not_last)
    def _():
        greet({"pix": pix + 1})

    band = band_matrix()
    fetch.wait()
    spread_image(own, table, chip, core)
    edge_rows[...] = jnp.zeros_like(edge_rows)
    for edge in range(2):
        for part in range(2):
            for k in range(3):
                start = table_row(chip, part, (3 if edge == 0 else 16) + k) + core * 4
                edge_rows[edge, pl.ds((part * 3 + k) * 4, 4), :] = table[pl.ds(start, 4), :]
    edges[...] = edge_rows[...].astype(BF)

    pl.semaphore_wait(barrier, MATES + not_first.astype(jnp.int32) + not_last.astype(jnp.int32))

    def to_strip(edge, strip):
        return pltpu.make_async_remote_copy(
            src_ref=edges.at[edge], dst_ref=from_strips.at[1 - edge], send_sem=pix_send.at[edge],
            recv_sem=pix_recv.at[1 - edge], device_id={"pix": strip}, device_id_type=MESH)

    def send(source, place, slot, send_sem, recv_sem, device):
        copy = pltpu.make_async_remote_copy(
            src_ref=source, dst_ref=place.at[slot], send_sem=send_sem,
            recv_sem=recv_sem.at[slot], device_id=device, device_id_type=MESH)
        copy.start()
        return copy

    @pl.when(not_first)
    def _():
        to_strip(0, pix - 1).start()

    @pl.when(not_last)
    def _():
        to_strip(1, pix + 1).start()

    sent = [send(own, blocks, MATES + core, block_send.at[0], block_recv, far_target)]
    for i, device in enumerate((mate(3), mate(2), mate(1), mate(0, 1))):
        sent.append(send(own, blocks, pj, block_send.at[1 + i], block_recv, device))

    @pl.when(not_first)
    def _():
        to_strip(1, pix - 1).wait_recv()

    @pl.when(not_last)
    def _():
        to_strip(0, pix + 1).wait_recv()

    @pl.when(jnp.logical_not(not_first))
    def _():
        from_strips[0] = jnp.zeros((32, COLS), BF)

    @pl.when(jnp.logical_not(not_last))
    def _():
        from_strips[1] = jnp.zeros((32, COLS), BF)

    both = jnp.concatenate([from_strips[edge].astype(F32)[:EDGE] for edge in range(2)], axis=0)
    halos[pj] = both.astype(BF)
    sent.append(send(halos.at[pj], halos, MATES + core, halo_send.at[0], halo_recv, far_target))
    for i, device in enumerate(mates):
        sent.append(send(halos.at[pj], halos, pj, halo_send.at[1 + i], halo_recv, device))

    def arrived(slot, place, sem):
        pltpu.make_async_remote_copy(
            src_ref=place.at[slot], dst_ref=place.at[slot], send_sem=sem.at[slot], recv_sem=sem.at[slot],
            device_id=mate(0, 1), device_id_type=MESH).wait_recv()

    for i in range(1, 4):
        slot = 2 * lax.rem(chip + i, 4) + core
        arrived(slot, blocks, block_recv)
        sent.append(send(blocks.at[slot], blocks, slot, pass_send.at[i], block_recv, mate(0, 1)))

    def take(group):
        def one(half, _):
            slot = group * 2 + half

            @pl.when(slot != pj)
            def _():
                @pl.when(jnp.logical_or(half != core, group == MATES // 2))
                def _():
                    arrived(slot, blocks, block_recv)

                spread_image(blocks.at[slot], table, group, half)
                arrived(slot, halos, halo_recv)

            spread_halo(halos.at[slot], table, group, half)
            return 0

        lax.fori_loop(0, 2, one, 0)
        inverse_root_power(table, scale, group, band)

    second = jnp.where(far, MATES // 2, lax.rem(pj, 4))
    take(second)

    def step(i, _):
        group = lax.rem(chip + i, 4)

        @pl.when(group != second)
        def _():
            take(group)

        def one(s, _):
            coherence_of(group * 8 + s, second, table, scale, stage, out, band)
            return 0

        lax.fori_loop(0, 8, one, 0, unroll=UNROLL)
        return 0

    lax.fori_loop(0, 4, step, 0)
    for copy in sent:
        copy.wait_send()

    @pl.when(not_first)
    def _():
        to_strip(0, pix - 1).wait_send()

    @pl.when(not_last)
    def _():
        to_strip(1, pix + 1).wait_send()


def per_device(images):
    return pl.pallas_call(
        kernel,
        out_shape=pltpu.VMEM((32, 8, 16, COLS), BF),
        in_specs=[pl.BlockSpec(memory_space=pltpu.HBM)],
        out_specs=pl.BlockSpec(memory_space=pltpu.VMEM),
        scratch_shapes=[
            pltpu.VMEM((2, 4, 16, COLS), BF),
            pltpu.VMEM((MATES + 2, 2, 4, 16, COLS), BF),
            pltpu.VMEM((MATES + 2, 2 * EDGE, COLS), BF),
            pltpu.VMEM((2, 32, COLS), BF),
            pltpu.VMEM((2, 32, COLS), BF),
            pltpu.VMEM((2, 32, COLS), F32),
            pltpu.VMEM((5 * 2 * WINDOW * 8, COLS), F32),
            pltpu.VMEM((5 * 128, COLS), F32),
            pltpu.VMEM((128, COLS), F32),
            pltpu.SemaphoreType.DMA,
            pltpu.SemaphoreType.DMA((2,)),
            pltpu.SemaphoreType.DMA((2,)),
            pltpu.SemaphoreType.DMA((5,)),
            pltpu.SemaphoreType.DMA((MATES + 2,)),
            pltpu.SemaphoreType.DMA((4,)),
            pltpu.SemaphoreType.DMA((MATES,)),
            pltpu.SemaphoreType.DMA((MATES + 2,)),
        ],
        compiler_params=pltpu.CompilerParams(
            collective_id=0, has_side_effects=True, vmem_limit_bytes=24 << 20
        ),
        name="coherence",
    )(pltpu.with_memory_space_constraint(images, pltpu.HBM))


def solution(mesh):
    return jax.shard_map(
        per_device,
        mesh=mesh,
        in_specs=(P(None, ("pi", "pj"), "pix", None),),
        out_specs=P("pi", "pj", "pix", None),
        check_vma=False,
    )
```

time: 30.9 us -> 19.4 us (0.63)
  the two profiles are of different devices: /device:TPU:24 before, /device:TPU:199 now
where the time goes in v2:
time: 19.4 us; the launch traced here: 19.3 us
  Pallas kernels  18.3 us (94%)
  local copies, waits for them, and re-layouts  0.97 us (5%)
    pallas_call x1, Pallas kernels, per_device(): pl.pallas_call(kernel, out_shape=pltpu.VMEM((32, 8, 16, COLS), BF), in_sp...  18.3 us
    unnamed x1, local copies, waits for them, and re-layouts  0.97 us

profile of v2, /device:TPU:199, one launch (start us, length us, event | category | flops | bytes accessed | tf_op | source)
XLA Modules:
  0.0 19.3 jit_solution(11430821726122319587)
XLA Ops:
  0.0 18.3 %coherence.1 = bf16[32,8,16,128]{3,2,1,0:T(8,128)(2,1)S(1)} custom-call(bf16[2,4,16,128]{3,2,1,0:T(8,128)(2,1)} %images.1), custom_call_target="tpu_custom_call" | custom-call | tf_op jit(solution)/shard_map/coherence/pallas_call | solution.py:253
  18.3 1.0 %copy.3 = bf16[32,8,16,128]{3,2,1,0:T(8,128)(2,1)} copy(bf16[32,8,16,128]{3,2,1,0:T(8,128)(2,1)S(1)} %coherence.1) | data formatting | bytes 2097152

commit v3 on v2

v3 whole, which is shorter than its diff:
```python
import jax
import jax.numpy as jnp
from jax import lax
from jax.experimental import pallas as pl
from jax.experimental.pallas import tpu as pltpu
from jax.sharding import PartitionSpec as P

BF = jnp.bfloat16
F32 = jnp.float32
MESH = pl.DeviceIdType.MESH
STRIP = 16
INNER = 10
COLS = 128
MATES = 8
EDGE = 24


def table_row(group, part, row):
    return ((group * 2 + part) * STRIP + row) * 8


def margin_row(group, part, row):
    return ((group * 2 + part) * 6 + row) * 8


def inner_sums(x):
    pairs = {j: x[j] + x[j + 1] for j in range(1, 15, 2)}
    full = []
    for s in range(0, 10, 2):
        middle = pairs[s + 1] + pairs[s + 3] + pairs[s + 5]
        full.append(x[s] + middle)
        full.append(middle + x[s + 7])
    first = (x[0] + pairs[1]) + x[3]
    second = first + x[4]
    last = (x[12] + pairs[13]) + x[15]
    before = x[11] + last
    return full, [first, second, second + x[5], x[10] + before, before, last]


def outer_sums(inside, x):
    above, below = x[1] + x[2], x[3] + x[4]
    return [
        inside[0] + (x[0] + above), inside[1] + above, inside[2] + x[2],
        inside[3] + x[3], inside[4] + below, inside[5] + (below + x[5]),
    ]


def sum_columns(rows, band):
    x = jnp.concatenate(rows, axis=0)
    high = x.astype(BF)
    low = (x - high.astype(F32)).astype(BF)
    return jnp.dot(jnp.concatenate([high, low], axis=1), band, preferred_element_type=F32)


def band_matrix():
    r = lax.broadcasted_iota(jnp.int32, (COLS, COLS), 0)
    c = lax.broadcasted_iota(jnp.int32, (COLS, COLS), 1)
    band = jnp.where(jnp.abs(r - c) <= 3, 1.0, 0.0).astype(BF)
    return jnp.concatenate([band, band], axis=0)


def spread_image(block, table, group, half):
    for part in range(2):
        for p in range(4):
            rows = block[part, p].astype(F32)
            for j in range(2):
                start = table_row(group, part, 8 * j) + half * 4 + p
                table[pl.ds(start, 8, stride=8), :] = rows[8 * j : 8 * j + 8]


def spread_halo(halo, margin, group, half):
    rows = halo[...].astype(F32)
    for edge in range(2):
        for part in range(2):
            for k in range(3):
                start = margin_row(group, part, 3 * edge + k) + half * 4
                first = EDGE * edge + (part * 3 + k) * 4
                margin[pl.ds(start, 4), :] = rows[first : first + 4]


def powers(load, rows):
    out = []
    for row in rows:
        a, b = load(0, row), load(1, row)
        out.append(a * a + b * b)
    return out


def products(first, second, rows):
    real, imag = [], []
    for row in rows:
        a = jnp.broadcast_to(first(0, row), (8, COLS))
        b = jnp.broadcast_to(first(1, row), (8, COLS))
        c, d = second(0, row), second(1, row)
        real.append(a * c + b * d)
        imag.append(b * c - a * d)
    return real, imag


def magnitude(x, y, first, second):
    q = x * x + y * y
    return (q * lax.rsqrt(jnp.maximum(q, 1e-36))) * (jnp.broadcast_to(first, (8, COLS)) * second)


def inner_scale(table, scale, group, band):
    full, _ = inner_sums(powers(lambda part, row: table[pl.ds(table_row(group, part, row), 8), :], range(STRIP)))
    scale[pl.ds(group * 8 * INNER, 8 * INNER), :] = lax.rsqrt(sum_columns(full, band))


def outer_scale(table, margin, scale, group, band):
    x = powers(lambda part, row: table[pl.ds(table_row(group, part, row), 8), :], range(STRIP))
    y = powers(lambda part, row: margin[pl.ds(margin_row(group, part, row), 8), :], range(6))
    scale[pl.ds(group * 8 * 6, 8 * 6), :] = lax.rsqrt(sum_columns(outer_sums(inner_sums(x)[1], y), band))


def inner_rows(group, s, second, table, scale, stage, inside, band):
    m = group * 8 + s
    real, imag = products(
        lambda part, row: table[pl.ds(table_row(group, part, row) + s, 1), :],
        lambda part, row: table[pl.ds(table_row(second, part, row), 8), :],
        range(STRIP),
    )
    real, real_inside = inner_sums(real)
    imag, imag_inside = inner_sums(imag)
    for i, value in enumerate(real_inside + imag_inside):
        inside[pl.ds((m * 12 + i) * 8, 8), :] = value
    w = sum_columns(real + imag, band)
    for r in range(INNER):
        value = magnitude(
            w[r * 8 : r * 8 + 8],
            w[(INNER + r) * 8 : (INNER + r) * 8 + 8],
            scale[pl.ds((group * INNER + r) * 8 + s, 1), :],
            scale[pl.ds((second * INNER + r) * 8, 8), :],
        )
        stage[pl.ds(m * 8 * STRIP + 3 + r, 8, stride=STRIP), :] = value


def outer_rows(base, s, second, margin, scale, stage, inside, edge_stage, out, band):
    group, m = base // 8, base + s
    real, imag = products(
        lambda part, row: margin[pl.ds(margin_row(group, part, row) + s, 1), :],
        lambda part, row: margin[pl.ds(margin_row(second, part, row), 8), :],
        range(6),
    )
    kept = [inside[pl.ds((m * 12 + i) * 8, 8), :] for i in range(12)]
    w = sum_columns(outer_sums(kept[:6], real) + outer_sums(kept[6:], imag), band)
    for i, r in enumerate((0, 1, 2, 5, 6, 7)):
        value = magnitude(
            w[i * 8 : i * 8 + 8],
            w[(6 + i) * 8 : (6 + i) * 8 + 8],
            scale[pl.ds((group * 6 + i) * 8 + s, 1), :],
            scale[pl.ds((second * 6 + i) * 8, 8), :],
        )
        edge_stage[pl.ds(r, 8, stride=8), :] = value
    row = lax.broadcasted_iota(jnp.int32, (8, COLS), 0)
    for n in range(8):
        edge = edge_stage[pl.ds(n * 8, 8), :]
        start = (m * 8 + n) * STRIP
        top = jnp.where(row < 3, edge, stage[pl.ds(start, 8), :])
        bottom = jnp.where(row > 4, edge, stage[pl.ds(start + 8, 8), :])
        out[m, n] = jnp.concatenate([top, bottom], axis=0).astype(BF)


def gather_kernel(images, table, halos, scale, stage, inside, own, blocks, edges, from_strips, edge_rows,
                  ready, own_sem, pix_send, pix_recv, block_send, block_recv, pass_send, halo_send, halo_recv):
    pi, pj, pix = lax.axis_index("pi"), lax.axis_index("pj"), lax.axis_index("pix")
    last = lax.axis_size("pix") - 1
    chip, core = pj // 2, lax.rem(pj, 2)
    far = (pj // 4) != pi
    not_first, not_last = pix > 0, pix < last

    def mate(chips, cores=0):
        return {"pj": 2 * lax.rem(chip + chips, 4) + lax.rem(core + cores, 2)}

    mates = [mate(3, 0), mate(3, 1), mate(2, 0), mate(2, 1), mate(1, 0), mate(1, 1), mate(0, 1)]
    far_target = {"pi": 1 - pi, "pj": 4 * pi + chip}

    fetch = pltpu.make_async_copy(images, own, own_sem)
    fetch.start()
    barrier = pltpu.get_barrier_semaphore()
    upper = pi == 1
    far_sources = [{"pi": 1 - pi, "pj": 2 * lax.rem(pj, 4) + c} for c in range(2)]

    def greet(device):
        pl.semaphore_signal(barrier, inc=1, device_id=device, device_id_type=MESH)

    @pl.when(jnp.logical_not(upper))
    def _():
        greet(far_target)

        @pl.when(far)
        def _():
            for device in far_sources:
                greet(device)

    for device in mates:
        greet(device)

    @pl.when(not_first)
    def _():
        greet({"pix": pix - 1})

    @pl.when(not_last)
    def _():
        greet({"pix": pix + 1})

    band = band_matrix()
    fetch.wait()
    def prepare():
        spread_image(own, table, chip, core)
        edge_rows[...] = jnp.zeros_like(edge_rows)
        for edge in range(2):
            for part in range(2):
                for k in range(3):
                    start = table_row(chip, part, (0 if edge == 0 else 13) + k) + core * 4
                    edge_rows[edge, pl.ds((part * 3 + k) * 4, 4), :] = table[pl.ds(start, 4), :]
        edges[...] = edge_rows[...].astype(BF)

    @pl.when(jnp.logical_not(upper))
    def _():
        prepare()

    strips = not_first.astype(jnp.int32) + not_last.astype(jnp.int32)
    from_lower = jnp.where(upper, jnp.where(far, 3, 1), 0)
    pl.semaphore_wait(barrier, MATES - 1 + strips + from_lower)

    @pl.when(jnp.logical_and(upper, far))
    def _():
        for device in far_sources:
            pl.semaphore_signal(ready, inc=1, device_id=device, device_id_type=MESH)


    def to_strip(edge, strip):
        return pltpu.make_async_remote_copy(
            src_ref=edges.at[edge], dst_ref=from_strips.at[1 - edge], send_sem=pix_send.at[edge],
            recv_sem=pix_recv.at[1 - edge], device_id={"pix": strip}, device_id_type=MESH)

    def send(source, place, slot, send_sem, recv_sem, device):
        copy = pltpu.make_async_remote_copy(
            src_ref=source, dst_ref=place.at[slot], send_sem=send_sem,
            recv_sem=recv_sem.at[slot], device_id=device, device_id_type=MESH)
        copy.start()
        return copy

    def to_far():
        return pltpu.make_async_remote_copy(
            src_ref=own, dst_ref=blocks.at[MATES + core], send_sem=block_send.at[0],
            recv_sem=block_recv.at[MATES + core], device_id=far_target, device_id_type=MESH)

    @pl.when(upper)
    def _():
        to_far().start()

    sent = [to_far()]
    for i, device in enumerate((mate(3), mate(2), mate(1), mate(0, 1))):
        sent.append(send(own, blocks, pj, block_send.at[1 + i], block_recv, device))

    @pl.when(upper)
    def _():
        prepare()

    @pl.when(not_first)
    def _():
        to_strip(0, pix - 1).start()

    @pl.when(not_last)
    def _():
        to_strip(1, pix + 1).start()

    @pl.when(jnp.logical_not(upper))
    def _():
        pl.semaphore_wait(ready, 1)
        to_far().start()

    @pl.when(not_first)
    def _():
        to_strip(1, pix - 1).wait_recv()

    @pl.when(not_last)
    def _():
        to_strip(0, pix + 1).wait_recv()

    @pl.when(jnp.logical_not(not_first))
    def _():
        from_strips[0] = jnp.zeros((32, COLS), BF)

    @pl.when(jnp.logical_not(not_last))
    def _():
        from_strips[1] = jnp.zeros((32, COLS), BF)

    both = jnp.concatenate([from_strips[edge].astype(F32)[:EDGE] for edge in range(2)], axis=0)
    halos[pj] = both.astype(BF)
    sent.append(send(halos.at[pj], halos, MATES + core, halo_send.at[0], halo_recv, far_target))
    for i, device in enumerate(mates):
        sent.append(send(halos.at[pj], halos, pj, halo_send.at[1 + i], halo_recv, device))

    def arrived(slot, place, sem):
        pltpu.make_async_remote_copy(
            src_ref=place.at[slot], dst_ref=place.at[slot], send_sem=sem.at[slot], recv_sem=sem.at[slot],
            device_id=mate(0, 1), device_id_type=MESH).wait_recv()

    for i in range(1, 4):
        slot = 2 * lax.rem(chip + i, 4) + core
        arrived(slot, blocks, block_recv)
        sent.append(send(blocks.at[slot], blocks, slot, pass_send.at[i], block_recv, mate(0, 1)))

    def take(group):
        def one(half, _):
            slot = group * 2 + half

            @pl.when(slot != pj)
            def _():
                @pl.when(jnp.logical_or(half != core, group == MATES // 2))
                def _():
                    arrived(slot, blocks, block_recv)

                spread_image(blocks.at[slot], table, group, half)

            return 0

        lax.fori_loop(0, 2, one, 0)
        inner_scale(table, scale, group, band)

    second = jnp.where(far, MATES // 2, lax.rem(pj, 4))

    @pl.when(far)
    def _():
        def early(i, _):
            take(lax.rem(chip + i, 4))
            return 0

        lax.fori_loop(0, 4, early, 0)

    take(second)

    def step(i, _):
        group = lax.rem(chip + i, 4)

        @pl.when(jnp.logical_not(jnp.logical_or(far, group == second)))
        def _():
            take(group)

        for s in range(8):
            inner_rows(group, s, second, table, scale, stage, inside, band)

        return 0

    lax.fori_loop(0, 4, step, 0)

    def halo_in(slot, _):
        @pl.when(slot != pj)
        def _():
            arrived(slot, halos, halo_recv)

        return 0

    lax.fori_loop(0, jnp.where(far, MATES + 2, MATES), halo_in, 0)
    for copy in sent:
        copy.wait_send()

    @pl.when(not_first)
    def _():
        to_strip(0, pix - 1).wait_send()

    @pl.when(not_last)
    def _():
        to_strip(1, pix + 1).wait_send()


def edge_kernel(table, halos, inner, stage, inside, result, margin, scale, edge_stage, out, out_sem):
    pi, pj = lax.axis_index("pi"), lax.axis_index("pj")
    far = (pj // 4) != pi
    second = jnp.where(far, MATES // 2, lax.rem(pj, 4))
    band = band_matrix()

    def take(group, _):
        for half in range(2):
            spread_halo(halos.at[group * 2 + half], margin, group, half)
        outer_scale(table, margin, scale, group, band)
        return 0

    for g in range(4):
        take(g, 0)

    @pl.when(far)
    def _():
        take(4, 0)

    def write(group):
        return pltpu.make_async_copy(
            out.at[pl.ds(group * 8, 8)], result.at[pl.ds(group * 8, 8)], out_sem.at[group])

    def step(group, _):
        for s in range(8):
            outer_rows(group * 8, s, second, margin, scale, stage, inside, edge_stage.at[group * 8 + s], out, band)
        write(group).start()
        return 0

    for g in range(4):
        step(g, 0)
    for group in range(4):
        write(group).wait()


def second_call(*kept):
    on_chip = pl.BlockSpec(memory_space=pltpu.VMEM)
    return pl.pallas_call(
        edge_kernel,
        out_shape=jax.ShapeDtypeStruct((32, 8, STRIP, COLS), BF),
        in_specs=[on_chip] * 5,
        out_specs=pl.BlockSpec(memory_space=pltpu.HBM),
        scratch_shapes=[
            pltpu.VMEM((5 * 2 * 6 * 8, COLS), F32),
            pltpu.VMEM((5 * 6 * 8, COLS), F32),
            pltpu.VMEM((32, 64, COLS), F32),
            pltpu.VMEM((32, 8, STRIP, COLS), BF),
            pltpu.SemaphoreType.DMA((4,)),
        ],
        compiler_params=pltpu.CompilerParams(vmem_limit_bytes=16 << 20),
        name="coherence_edges",
    )(*kept)


def per_device(images):
    on_chip = pl.BlockSpec(memory_space=pltpu.VMEM)
    kept = pl.pallas_call(
        gather_kernel,
        out_shape=(
            pltpu.VMEM((5 * 2 * STRIP * 8, COLS), F32),
            pltpu.VMEM((MATES + 2, 2 * EDGE, COLS), BF),
            pltpu.VMEM((5 * INNER * 8, COLS), F32),
            pltpu.VMEM((32 * 8 * STRIP, COLS), F32),
            pltpu.VMEM((32 * 12 * 8, COLS), F32),
        ),
        in_specs=[pl.BlockSpec(memory_space=pltpu.HBM)],
        out_specs=(on_chip,) * 5,
        scratch_shapes=[
            pltpu.VMEM((2, 4, 16, COLS), BF),
            pltpu.VMEM((MATES + 2, 2, 4, 16, COLS), BF),
            pltpu.VMEM((2, 32, COLS), BF),
            pltpu.VMEM((2, 32, COLS), BF),
            pltpu.VMEM((2, 32, COLS), F32),
            pltpu.SemaphoreType.REGULAR,
            pltpu.SemaphoreType.DMA,
            pltpu.SemaphoreType.DMA((2,)),
            pltpu.SemaphoreType.DMA((2,)),
            pltpu.SemaphoreType.DMA((5,)),
            pltpu.SemaphoreType.DMA((MATES + 2,)),
            pltpu.SemaphoreType.DMA((4,)),
            pltpu.SemaphoreType.DMA((MATES,)),
            pltpu.SemaphoreType.DMA((MATES + 2,)),
        ],
        compiler_params=pltpu.CompilerParams(
            collective_id=0, has_side_effects=True, vmem_limit_bytes=16 << 20
        ),
        name="coherence_inner",
    )(pltpu.with_memory_space_constraint(images, pltpu.HBM))
    return second_call(*kept)


def solution(mesh):
    return jax.shard_map(
        per_device,
        mesh=mesh,
        in_specs=(P(None, ("pi", "pj"), "pix", None),),
        out_specs=P("pi", "pj", "pix", None),
        check_vma=False,
    )
```

time: 19.4 us -> 19.7 us (1.015)
  the two profiles are of different devices: /device:TPU:199 before, /device:TPU:1 now
where the time goes in v3:
time: 19.7 us; the launch traced here: 19.5 us
  Pallas kernels  19.5 us (99%)
    pallas_call x1, Pallas kernels, per_device(): pl.pallas_call(gather_kernel, out_shape=(pltpu.VMEM((5 * 2 * STRIP * 8, C...  17.6 us
    pallas_call x1, Pallas kernels, second_call(): pl.pallas_call(edge_kernel, out_shape=jax.ShapeDtypeStruct((32, 8, STRIP,...  1.91 us

profile of v3, /device:TPU:1, one launch (start us, length us, event | category | flops | bytes accessed | tf_op | source)
XLA Modules:
  0.0 19.5 jit_solution(11270854092654188775)
XLA Ops:
  0.0 17.6 %coherence_inner.1 = (f32[1280,128]{1,0:T(8,128)S(1)}, bf16[10,48,128]{2,1,0:T(8,128)(2,1)S(1)}, f32[400,128]{1,0:T(8,128)S(1)}, f32[4096,128]{1,0:T(8,128)S(1)}, f32[3072,128]{1,0:T(8,128)S(1)}) custom-call(bf16[2,4,16,128]{3,2,1,0:T(8,128)(2,1)} %images.1), custom_call_target="tpu_custom_call" | custom-call | tf_op jit(solution)/shard_map/coherence_inner/pallas_call | solution.py:426
  17.6 1.9 %coherence_edges.1 = bf16[32,8,16,128]{3,2,1,0:T(8,128)(2,1)} custom-call(f32[1280,128]{1,0:T(8,128)S(1)} %get-tuple-element.10.table, bf16[10,48,128]{2,1,0:T(8,128)(2,1)S(1)} %get-tuple-element.11.halos, f32[400,128]{1,0:T(8,128)S(1)} %get-tuple-element.12.inner, f32[4096,128]{1,0:T(8,128)S(1)} %get-tuple-element.13.stage, ...), custom_call_target="tpu_custom_call" | custom-call | tf_op jit(solution)/shard_map/coherence_edges/pallas_call | solution.py:407

commit v4 on v3

--- a/solution.py
+++ b/solution.py
@@ -162,50 +162,71 @@
 
 
 def gather_kernel(images, table, halos, scale, stage, inside, own, blocks, edges, from_strips, edge_rows,
-                  ready, own_sem, pix_send, pix_recv, block_send, block_recv, pass_send, halo_send, halo_recv):
+                  ready, late, own_sem, pix_send, pix_recv, block_send, block_recv, pass_send, halo_send, halo_recv,
+                  hand_send, pass_halo):
     pi, pj, pix = lax.axis_index("pi"), lax.axis_index("pj"), lax.axis_index("pix")
     last = lax.axis_size("pix") - 1
     chip, core = pj // 2, lax.rem(pj, 2)
     far = (pj // 4) != pi
+    upper = pi == 1
+    lower = jnp.logical_not(upper)
     not_first, not_last = pix > 0, pix < last
+
+    def both(a, b):
+        return jnp.logical_and(a, b)
+
+    first_column = both(lower, pix == 0)
+    corner = both(first_column, pj == 0)
+    corner_mate = both(first_column, pj != 0)
+    sibling = both(first_column, pj == 1)
+    corner_strip = both(lower, both(pix == 1, pj == 0))
+    corner_far = both(upper, both(pix == 0, pj == 0))
+
+    def number(condition):
+        return condition.astype(jnp.int32)
 
     def mate(chips, cores=0):
         return {"pj": 2 * lax.rem(chip + chips, 4) + lax.rem(core + cores, 2)}
 
     mates = [mate(3, 0), mate(3, 1), mate(2, 0), mate(2, 1), mate(1, 0), mate(1, 1), mate(0, 1)]
     far_target = {"pi": 1 - pi, "pj": 4 * pi + chip}
+    far_sources = [{"pi": 1 - pi, "pj": 2 * lax.rem(pj, 4) + c} for c in range(2)]
 
     fetch = pltpu.make_async_copy(images, own, own_sem)
     fetch.start()
     barrier = pltpu.get_barrier_semaphore()
-    upper = pi == 1
-    far_sources = [{"pi": 1 - pi, "pj": 2 * lax.rem(pj, 4) + c} for c in range(2)]
 
     def greet(device):
         pl.semaphore_signal(barrier, inc=1, device_id=device, device_id_type=MESH)
 
-    @pl.when(jnp.logical_not(upper))
-    def _():
-        greet(far_target)
-
-        @pl.when(far)
-        def _():
-            for device in far_sources:
-                greet(device)
-
-    for device in mates:
-        greet(device)
-
-    @pl.when(not_first)
-    def _():
-        greet({"pix": pix - 1})
-
-    @pl.when(not_last)
-    def _():
-        greet({"pix": pix + 1})
+    @pl.when(jnp.logical_not(corner))
+    def _():
+        @pl.when(lower)
+        def _():
+            greet(far_target)
+
+            @pl.when(far)
+            def _():
+                for device in far_sources:
+                    greet(device)
+
+        for device in mates:
+            greet(device)
+
+        @pl.when(corner_far)
+        def _():
+            greet(far_sources[0])
+
+        @pl.when(not_first)
+        def _():
+            greet({"pix": pix - 1})
+
+        @pl.when(not_last)
+        def _():
+            greet({"pix": pix + 1})
 
     band = band_matrix()
-    fetch.wait()
+
     def prepare():
         spread_image(own, table, chip, core)
         edge_rows[...] = jnp.zeros_like(edge_rows)
@@ -216,93 +237,151 @@
                     edge_rows[edge, pl.ds((part * 3 + k) * 4, 4), :] = table[pl.ds(start, 4), :]
         edges[...] = edge_rows[...].astype(BF)
 
-    @pl.when(jnp.logical_not(upper))
-    def _():
+    @pl.when(lower)
+    def _():
+        fetch.wait()
         prepare()
 
-    strips = not_first.astype(jnp.int32) + not_last.astype(jnp.int32)
     from_lower = jnp.where(upper, jnp.where(far, 3, 1), 0)
-    pl.semaphore_wait(barrier, MATES - 1 + strips + from_lower)
-
-    @pl.when(jnp.logical_and(upper, far))
-    def _():
-        for device in far_sources:
-            pl.semaphore_signal(ready, inc=1, device_id=device, device_id_type=MESH)
-
+    greetings = MATES - 1 + number(not_first) + number(not_last) + from_lower
+    pl.semaphore_wait(
+        barrier, greetings + number(corner) - number(corner_mate) - number(corner_strip) - number(corner_far))
+
+    @pl.when(both(upper, far))
+    def _():
+        @pl.when(jnp.logical_not(corner_far))
+        def _():
+            pl.semaphore_signal(ready, inc=1, device_id=far_sources[0], device_id_type=MESH)
+
+        pl.semaphore_signal(ready, inc=1, device_id=far_sources[1], device_id_type=MESH)
+
+    @pl.when(corner)
+    def _():
+        for device in ({"pj": 1}, {"pix": 1}):
+            pl.semaphore_signal(late, inc=1, device_id=device, device_id_type=MESH)
 
     def to_strip(edge, strip):
         return pltpu.make_async_remote_copy(
             src_ref=edges.at[edge], dst_ref=from_strips.at[1 - edge], send_sem=pix_send.at[edge],
             recv_sem=pix_recv.at[1 - edge], device_id={"pix": strip}, device_id_type=MESH)
 
-    def send(source, place, slot, send_sem, recv_sem, device):
-        copy = pltpu.make_async_remote_copy(
+    def sending(source, place, slot, send_sem, recv_sem, device):
+        return pltpu.make_async_remote_copy(
             src_ref=source, dst_ref=place.at[slot], send_sem=send_sem,
             recv_sem=recv_sem.at[slot], device_id=device, device_id_type=MESH)
-        copy.start()
-        return copy
-
-    def to_far():
-        return pltpu.make_async_remote_copy(
-            src_ref=own, dst_ref=blocks.at[MATES + core], send_sem=block_send.at[0],
-            recv_sem=block_recv.at[MATES + core], device_id=far_target, device_id_type=MESH)
+
+    sent = []
+
+    def is_corner(device):
+        return both(corner_mate, device["pj"] == 0)
+
+    def send(copy, condition):
+        @pl.when(condition)
+        def _():
+            copy.start()
+
+    def send_to_mates(source, place, send_sem, recv_sem):
+        for i, device in enumerate((mate(3), mate(2), mate(1), mate(0, 1))):
+            target = jnp.where(both(is_corner(device), pj != 1), 1, device["pj"])
+            copy = sending(source, place, pj, send_sem.at[1 + i], recv_sem, {"pj": target})
+            send(copy, jnp.logical_not(both(sibling, target == 0)))
+            sent.append(copy)
+
+    to_far = sending(own, blocks, MATES + core, block_send.at[0], block_recv, far_target)
+    sent.append(to_far)
 
     @pl.when(upper)
     def _():
-        to_far().start()
-
-    sent = [to_far()]
-    for i, device in enumerate((mate(3), mate(2), mate(1), mate(0, 1))):
-        sent.append(send(own, blocks, pj, block_send.at[1 + i], block_recv, device))
+        fetch.wait()
+
+    @pl.when(jnp.logical_or(upper, corner))
+    def _():
+        to_far.start()
+
+    send_to_mates(own, blocks, block_send, block_recv)
 
     @pl.when(upper)
     def _():
         prepare()
 
+    @pl.when(both(not_first, jnp.logical_not(corner_strip)))
+    def _():
+        to_strip(0, pix - 1).start()
+
+    @pl.when(not_last)
+    def _():
+        to_strip(1, pix + 1).start()
+
+    @pl.when(both(lower, jnp.logical_not(corner)))
+    def _():
+        pl.semaphore_wait(ready, 1)
+        to_far.start()
+
+    def arrived(slot, place, sem):
+        sending(place.at[slot], place, slot, sem.at[slot], sem, mate(0, 1)).wait_recv()
+
     @pl.when(not_first)
     def _():
+        to_strip(1, pix - 1).wait_recv()
+
+    @pl.when(not_last)
+    def _():
+        to_strip(0, pix + 1).wait_recv()
+
+    @pl.when(jnp.logical_not(not_first))
+    def _():
+        from_strips[0] = jnp.zeros((32, COLS), BF)
+
+    @pl.when(jnp.logical_not(not_last))
+    def _():
+        from_strips[1] = jnp.zeros((32, COLS), BF)
+
+    rows = jnp.concatenate([from_strips[edge].astype(F32)[:EDGE] for edge in range(2)], axis=0)
+    halos[pj] = rows.astype(BF)
+    far_halo = sending(halos.at[pj], halos, MATES + core, halo_send.at[0], halo_recv, far_target)
+    far_halo.start()
+    sent.append(far_halo)
+    send_to_mates(halos.at[pj], halos, halo_send, halo_recv)
+
+    def hand_over(i, place, send_sem, recv_sem):
+        slot = 2 * lax.rem(chip + i, 4) + core
+        return slot, sending(place.at[slot], place, slot, send_sem.at[i], recv_sem, mate(0, 1))
+
+    def hand_all_over(place, send_sem, recv_sem):
+        for i in range(1, 4):
+            slot, copy = hand_over(i, place, send_sem, recv_sem)
+
+            @pl.when(jnp.logical_not(jnp.logical_or(corner, both(corner_mate, slot == 0))))
+            def _():
+                arrived(slot, place, recv_sem)
+                send(copy, jnp.logical_not(sibling))
+
+    def hand_corner_over(place, send_sem, recv_sem):
+        for i in range(1, 4):
+            slot, copy = hand_over(i, place, send_sem, recv_sem)
+
+            @pl.when(both(corner_mate, slot == 0))
+            def _():
+                arrived(slot, place, recv_sem)
+                copy.start()
+
+    hand_all_over(blocks, pass_send, block_recv)
+
+    @pl.when(corner_strip)
+    def _():
+        pl.semaphore_wait(late, 1)
         to_strip(0, pix - 1).start()
 
-    @pl.when(not_last)
-    def _():
-        to_strip(1, pix + 1).start()
-
-    @pl.when(jnp.logical_not(upper))
-    def _():
-        pl.semaphore_wait(ready, 1)
-        to_far().start()
-
-    @pl.when(not_first)
-    def _():
-        to_strip(1, pix - 1).wait_recv()
-
-    @pl.when(not_last)
-    def _():
-        to_strip(0, pix + 1).wait_recv()
-
-    @pl.when(jnp.logical_not(not_first))
-    def _():
-        from_strips[0] = jnp.zeros((32, COLS), BF)
-
-    @pl.when(jnp.logical_not(not_last))
-    def _():
-        from_strips[1] = jnp.zeros((32, COLS), BF)
-
-    both = jnp.concatenate([from_strips[edge].astype(F32)[:EDGE] for edge in range(2)], axis=0)
-    halos[pj] = both.astype(BF)
-    sent.append(send(halos.at[pj], halos, MATES + core, halo_send.at[0], halo_recv, far_target))
-    for i, device in enumerate(mates):
-        sent.append(send(halos.at[pj], halos, pj, halo_send.at[1 + i], halo_recv, device))
-
-    def arrived(slot, place, sem):
-        pltpu.make_async_remote_copy(
-            src_ref=place.at[slot], dst_ref=place.at[slot], send_sem=sem.at[slot], recv_sem=sem.at[slot],
-            device_id=mate(0, 1), device_id_type=MESH).wait_recv()
-
-    for i in range(1, 4):
-        slot = 2 * lax.rem(chip + i, 4) + core
-        arrived(slot, blocks, block_recv)
-        sent.append(send(blocks.at[slot], blocks, slot, pass_send.at[i], block_recv, mate(0, 1)))
+    def to_corner(slot, place, sem, send_sem):
+        return sending(place.at[slot], place, slot, send_sem, sem, {"pj": 0})
+
+    def serve_corner():
+        pl.semaphore_wait(late, 1)
+        sending(own, blocks, pj, block_send.at[4], block_recv, {"pj": 0}).start()
+        sending(halos.at[pj], halos, pj, halo_send.at[4], halo_recv, {"pj": 0}).start()
+        for i in range(1, 4):
+            hand_over(i, blocks, pass_send, block_recv)[1].start()
+            to_corner(2 * i, blocks, block_recv, pass_send.at[3 + i]).start()
 
     def take(group):
         def one(half, _):
@@ -310,7 +389,7 @@
 
             @pl.when(slot != pj)
             def _():
-                @pl.when(jnp.logical_or(half != core, group == MATES // 2))
+                @pl.when(jnp.logical_or(corner, jnp.logical_or(half != core, group == MATES // 2)))
                 def _():
                     arrived(slot, blocks, block_recv)
 
@@ -321,22 +400,43 @@
         lax.fori_loop(0, 2, one, 0)
         inner_scale(table, scale, group, band)
 
+    def group_at(i):
+        ahead = lax.rem(chip + i + number(both(corner_mate, chip == 0)), 4)
+        return jnp.where(chip < 2, ahead, jnp.where(both(chip == 2, i < 2), 2 + i, 3 - i))
+
     second = jnp.where(far, MATES // 2, lax.rem(pj, 4))
 
-    @pl.when(far)
+    eager = jnp.logical_or(far, sibling)
+
+    @pl.when(eager)
     def _():
         def early(i, _):
-            take(lax.rem(chip + i, 4))
+            take(group_at(i))
             return 0
 
-        lax.fori_loop(0, 4, early, 0)
-
-    take(second)
+        lax.fori_loop(0, 4 - number(corner_mate), early, 0)
+
+    @pl.when(sibling)
+    def _():
+        serve_corner()
+
+
+    @pl.when(jnp.logical_not(sibling))
+    def _():
+        take(second)
 
     def step(i, _):
-        group = lax.rem(chip + i, 4)
-
-        @pl.when(jnp.logical_not(jnp.logical_or(far, group == second)))
+        group = group_at(i)
+
+        @pl.when(i == 2)
+        def _():
+            hand_all_over(halos, pass_halo, halo_recv)
+
+        @pl.when(i == 3)
+        def _():
+            hand_corner_over(blocks, pass_send, block_recv)
+
+        @pl.when(jnp.logical_or(both(jnp.logical_not(eager), group != second), both(eager, both(corner_mate, i == 3))))
         def _():
             take(group)
 
@@ -350,13 +450,37 @@
     def halo_in(slot, _):
         @pl.when(slot != pj)
         def _():
-            arrived(slot, halos, halo_recv)
+            @pl.when(jnp.logical_or(corner, jnp.logical_or(lax.rem(slot, 2) != core, slot >= MATES)))
+            def _():
+                arrived(slot, halos, halo_recv)
+
+            @pl.when(both(sibling, slot > 1))
+            def _():
+                to_corner(slot, halos, halo_recv, hand_send.at[slot]).start()
 
         return 0
 
     lax.fori_loop(0, jnp.where(far, MATES + 2, MATES), halo_in, 0)
+    hand_corner_over(halos, pass_halo, halo_recv)
     for copy in sent:
         copy.wait_send()
+
+    @pl.when(jnp.logical_not(corner))
+    def _():
+        for i in range(1, 4):
+            hand_over(i, blocks, pass_send, block_recv)[1].wait_send()
+
+    @pl.when(jnp.logical_not(jnp.logical_or(corner, sibling)))
+    def _():
+        for i in range(1, 4):
+            hand_over(i, halos, pass_halo, halo_recv)[1].wait_send()
+
+    @pl.when(sibling)
+    def _():
+        for i in range(1, 4):
+            to_corner(2 * i, blocks, block_recv, pass_send.at[3 + i]).wait_send()
+        for slot in range(2, MATES):
+            to_corner(slot, halos, halo_recv, hand_send.at[slot]).wait_send()
 
     @pl.when(not_first)
     def _():
@@ -441,14 +565,17 @@
             pltpu.VMEM((2, 32, COLS), BF),
             pltpu.VMEM((2, 32, COLS), F32),
             pltpu.SemaphoreType.REGULAR,
+            pltpu.SemaphoreType.REGULAR,
             pltpu.SemaphoreType.DMA,
             pltpu.SemaphoreType.DMA((2,)),
             pltpu.SemaphoreType.DMA((2,)),
             pltpu.SemaphoreType.DMA((5,)),
             pltpu.SemaphoreType.DMA((MATES + 2,)),
+            pltpu.SemaphoreType.DMA((7,)),
+            pltpu.SemaphoreType.DMA((5,)),
+            pltpu.SemaphoreType.DMA((MATES + 2,)),
+            pltpu.SemaphoreType.DMA((MATES,)),
             pltpu.SemaphoreType.DMA((4,)),
-            pltpu.SemaphoreType.DMA((MATES,)),
-            pltpu.SemaphoreType.DMA((MATES + 2,)),
         ],
         compiler_params=pltpu.CompilerParams(
             collective_id=0, has_side_effects=True, vmem_limit_bytes=16 << 20

time: 19.7 us -> 18.8 us (0.954)
  the two profiles are of different devices: /device:TPU:1 before, /device:TPU:238 now
where the time goes in v4:
time: 18.8 us; the launch traced here: 18.6 us
  Pallas kernels  18.6 us (99%)
    pallas_call x1, Pallas kernels, per_device(): pl.pallas_call(gather_kernel, out_shape=(pltpu.VMEM((5 * 2 * STRIP * 8, C...  16.6 us
    pallas_call x1, Pallas kernels, second_call(): pl.pallas_call(edge_kernel, out_shape=jax.ShapeDtypeStruct((32, 8, STRIP,...  2.04 us

profile of v4, /device:TPU:238, one launch (start us, length us, event | category | flops | bytes accessed | tf_op | source)
XLA Modules:
  0.0 18.6 jit_solution(14790917959298885855)
XLA Ops:
  0.0 16.6 %coherence_inner.1 = (f32[1280,128]{1,0:T(8,128)S(1)}, bf16[10,48,128]{2,1,0:T(8,128)(2,1)S(1)}, f32[400,128]{1,0:T(8,128)S(1)}, f32[4096,128]{1,0:T(8,128)S(1)}, f32[3072,128]{1,0:T(8,128)S(1)}) custom-call(bf16[2,4,16,128]{3,2,1,0:T(8,128)(2,1)} %images.1), custom_call_target="tpu_custom_call" | custom-call | tf_op jit(solution)/shard_map/coherence_inner/pallas_call | solution.py:550
  16.6 2.0 %coherence_edges.1 = bf16[32,8,16,128]{3,2,1,0:T(8,128)(2,1)} custom-call(f32[1280,128]{1,0:T(8,128)S(1)} %get-tuple-element.10.table, bf16[10,48,128]{2,1,0:T(8,128)(2,1)S(1)} %get-tuple-element.11.halos, f32[400,128]{1,0:T(8,128)S(1)} %get-tuple-element.12.inner, f32[4096,128]{1,0:T(8,128)S(1)} %get-tuple-element.13.stage, ...), custom_call_target="tpu_custom_call" | custom-call | tf_op jit(solution)/shard_map/coherence_edges/pallas_call | solution.py:531

commit v5 on v4

--- a/solution.py
+++ b/solution.py
@@ -107,8 +107,8 @@
     scale[pl.ds(group * 8 * INNER, 8 * INNER), :] = lax.rsqrt(sum_columns(full, band))
 
 
-def outer_scale(table, margin, scale, group, band):
-    x = powers(lambda part, row: table[pl.ds(table_row(group, part, row), 8), :], range(STRIP))
+def outer_scale(table, margin, scale, group, source, band):
+    x = powers(lambda part, row: table[pl.ds(table_row(source, part, row), 8), :], range(STRIP))
     y = powers(lambda part, row: margin[pl.ds(margin_row(group, part, row), 8), :], range(6))
     scale[pl.ds(group * 8 * 6, 8 * 6), :] = lax.rsqrt(sum_columns(outer_sums(inner_sums(x)[1], y), band))
 
@@ -135,11 +135,11 @@
         stage[pl.ds(m * 8 * STRIP + 3 + r, 8, stride=STRIP), :] = value
 
 
-def outer_rows(base, s, second, margin, scale, stage, inside, edge_stage, out, band):
-    group, m = base // 8, base + s
+def outer_rows(group, s, margin, scale, stage, inside, edge_stage, out, band):
+    m = group * 8 + s
     real, imag = products(
         lambda part, row: margin[pl.ds(margin_row(group, part, row) + s, 1), :],
-        lambda part, row: margin[pl.ds(margin_row(second, part, row), 8), :],
+        lambda part, row: margin[pl.ds(margin_row(4, part, row), 8), :],
         range(6),
     )
     kept = [inside[pl.ds((m * 12 + i) * 8, 8), :] for i in range(12)]
@@ -149,7 +149,7 @@
             w[i * 8 : i * 8 + 8],
             w[(6 + i) * 8 : (6 + i) * 8 + 8],
             scale[pl.ds((group * 6 + i) * 8 + s, 1), :],
-            scale[pl.ds((second * 6 + i) * 8, 8), :],
+            scale[pl.ds((4 * 6 + i) * 8, 8), :],
         )
         edge_stage[pl.ds(r, 8, stride=8), :] = value
     row = lax.broadcasted_iota(jnp.int32, (8, COLS), 0)
@@ -162,7 +162,7 @@
 
 
 def gather_kernel(images, table, halos, scale, stage, inside, own, blocks, edges, from_strips, edge_rows,
-                  ready, late, own_sem, pix_send, pix_recv, block_send, block_recv, pass_send, halo_send, halo_recv,
+                  ready, late, next_ready, own_sem, pix_send, pix_recv, block_send, block_recv, pass_send, halo_send, halo_recv,
                   hand_send, pass_halo):
     pi, pj, pix = lax.axis_index("pi"), lax.axis_index("pj"), lax.axis_index("pix")
     last = lax.axis_size("pix") - 1
@@ -182,6 +182,9 @@
     corner_strip = both(lower, both(pix == 1, pj == 0))
     corner_far = both(upper, both(pix == 0, pj == 0))
 
+    before_step = both(not_last, both(upper, lax.rem(pix, 4) != 3))
+    after_step = both(not_first, both(upper, lax.rem(pix, 4) != 0))
+
     def number(condition):
         return condition.astype(jnp.int32)
 
@@ -217,7 +220,7 @@
         def _():
             greet(far_sources[0])
 
-        @pl.when(not_first)
+        @pl.when(both(not_first, jnp.logical_not(after_step)))
         def _():
             greet({"pix": pix - 1})
 
@@ -237,7 +240,7 @@
                     edge_rows[edge, pl.ds((part * 3 + k) * 4, 4), :] = table[pl.ds(start, 4), :]
         edges[...] = edge_rows[...].astype(BF)
 
-    @pl.when(lower)
+    @pl.when(jnp.logical_not(corner))
     def _():
         fetch.wait()
         prepare()
@@ -245,7 +248,8 @@
     from_lower = jnp.where(upper, jnp.where(far, 3, 1), 0)
     greetings = MATES - 1 + number(not_first) + number(not_last) + from_lower
     pl.semaphore_wait(
-        barrier, greetings + number(corner) - number(corner_mate) - number(corner_strip) - number(corner_far))
+        barrier, greetings + number(corner) - number(corner_mate) - number(corner_strip) - number(corner_far)
+        - number(before_step))
 
     @pl.when(both(upper, far))
     def _():
@@ -254,6 +258,10 @@
             pl.semaphore_signal(ready, inc=1, device_id=far_sources[0], device_id_type=MESH)
 
         pl.semaphore_signal(ready, inc=1, device_id=far_sources[1], device_id_type=MESH)
+
+    @pl.when(after_step)
+    def _():
+        pl.semaphore_signal(next_ready, inc=1, device_id={"pix": pix - 1}, device_id_type=MESH)
 
     @pl.when(corner)
     def _():
@@ -270,7 +278,7 @@
             src_ref=source, dst_ref=place.at[slot], send_sem=send_sem,
             recv_sem=recv_sem.at[slot], device_id=device, device_id_type=MESH)
 
-    sent = []
+    sent, sent_by_corner = [], []
 
     def is_corner(device):
         return both(corner_mate, device["pj"] == 0)
@@ -286,11 +294,15 @@
             copy = sending(source, place, pj, send_sem.at[1 + i], recv_sem, {"pj": target})
             send(copy, jnp.logical_not(both(sibling, target == 0)))
             sent.append(copy)
+        for i in range(1, 4):
+            copy = sending(source, place, pj, send_sem.at[4 + i], recv_sem, mate(i, 1))
+            send(copy, corner)
+            sent_by_corner.append(copy)
 
     to_far = sending(own, blocks, MATES + core, block_send.at[0], block_recv, far_target)
     sent.append(to_far)
 
-    @pl.when(upper)
+    @pl.when(corner)
     def _():
         fetch.wait()
 
@@ -300,7 +312,7 @@
 
     send_to_mates(own, blocks, block_send, block_recv)
 
-    @pl.when(upper)
+    @pl.when(corner)
     def _():
         prepare()
 
@@ -308,7 +320,7 @@
     def _():
         to_strip(0, pix - 1).start()
 
-    @pl.when(not_last)
+    @pl.when(both(not_last, jnp.logical_not(before_step)))
     def _():
         to_strip(1, pix + 1).start()
 
@@ -316,6 +328,11 @@
     def _():
         pl.semaphore_wait(ready, 1)
         to_far.start()
+
+    @pl.when(before_step)
+    def _():
+        pl.semaphore_wait(next_ready, 1)
+        to_strip(1, pix + 1).start()
 
     def arrived(slot, place, sem):
         sending(place.at[slot], place, slot, sem.at[slot], sem, mate(0, 1)).wait_recv()
@@ -343,6 +360,9 @@
     sent.append(far_halo)
     send_to_mates(halos.at[pj], halos, halo_send, halo_recv)
 
+    def not_handed(slot):
+        return jnp.logical_or(corner, both(corner_mate, slot == 0))
+
     def hand_over(i, place, send_sem, recv_sem):
         slot = 2 * lax.rem(chip + i, 4) + core
         return slot, sending(place.at[slot], place, slot, send_sem.at[i], recv_sem, mate(0, 1))
@@ -351,19 +371,10 @@
         for i in range(1, 4):
             slot, copy = hand_over(i, place, send_sem, recv_sem)
 
-            @pl.when(jnp.logical_not(jnp.logical_or(corner, both(corner_mate, slot == 0))))
+            @pl.when(jnp.logical_not(not_handed(slot)))
             def _():
                 arrived(slot, place, recv_sem)
                 send(copy, jnp.logical_not(sibling))
-
-    def hand_corner_over(place, send_sem, recv_sem):
-        for i in range(1, 4):
-            slot, copy = hand_over(i, place, send_sem, recv_sem)
-
-            @pl.when(both(corner_mate, slot == 0))
-            def _():
-                arrived(slot, place, recv_sem)
-                copy.start()
 
     hand_all_over(blocks, pass_send, block_recv)
 
@@ -389,7 +400,7 @@
 
             @pl.when(slot != pj)
             def _():
-                @pl.when(jnp.logical_or(corner, jnp.logical_or(half != core, group == MATES // 2)))
+                @pl.when(jnp.logical_or(not_handed(slot), jnp.logical_or(half != core, group == MATES // 2)))
                 def _():
                     arrived(slot, blocks, block_recv)
 
@@ -406,51 +417,40 @@
 
     second = jnp.where(far, MATES // 2, lax.rem(pj, 4))
 
-    eager = jnp.logical_or(far, sibling)
-
-    @pl.when(eager)
-    def _():
-        def early(i, _):
-            take(group_at(i))
-            return 0
-
-        lax.fori_loop(0, 4 - number(corner_mate), early, 0)
-
-    @pl.when(sibling)
-    def _():
-        serve_corner()
-
-
-    @pl.when(jnp.logical_not(sibling))
-    def _():
-        take(second)
-
-    def step(i, _):
+    def early(i, _):
+        take(group_at(i))
+        return 0
+
+    def pairs(i):
         group = group_at(i)
-
-        @pl.when(i == 2)
-        def _():
-            hand_all_over(halos, pass_halo, halo_recv)
-
-        @pl.when(i == 3)
-        def _():
-            hand_corner_over(blocks, pass_send, block_recv)
-
-        @pl.when(jnp.logical_or(both(jnp.logical_not(eager), group != second), both(eager, both(corner_mate, i == 3))))
-        def _():
-            take(group)
-
         for s in range(8):
             inner_rows(group, s, second, table, scale, stage, inside, band)
 
-        return 0
-
-    lax.fori_loop(0, 4, step, 0)
+    lax.fori_loop(0, 4 - number(corner_mate), early, 0)
+
+    @pl.when(sibling)
+    def _():
+        serve_corner()
+
+    @pl.when(far)
+    def _():
+        take(second)
+
+    pairs(0)
+    pairs(1)
+    hand_all_over(halos, pass_halo, halo_recv)
+    pairs(2)
+
+    @pl.when(corner_mate)
+    def _():
+        take(group_at(3))
+
+    pairs(3)
 
     def halo_in(slot, _):
         @pl.when(slot != pj)
         def _():
-            @pl.when(jnp.logical_or(corner, jnp.logical_or(lax.rem(slot, 2) != core, slot >= MATES)))
+            @pl.when(jnp.logical_or(not_handed(slot), jnp.logical_or(lax.rem(slot, 2) != core, slot >= MATES)))
             def _():
                 arrived(slot, halos, halo_recv)
 
@@ -461,19 +461,25 @@
         return 0
 
     lax.fori_loop(0, jnp.where(far, MATES + 2, MATES), halo_in, 0)
-    hand_corner_over(halos, pass_halo, halo_recv)
     for copy in sent:
         copy.wait_send()
 
+    @pl.when(corner)
+    def _():
+        for copy in sent_by_corner:
+            copy.wait_send()
+
     @pl.when(jnp.logical_not(corner))
     def _():
         for i in range(1, 4):
-            hand_over(i, blocks, pass_send, block_recv)[1].wait_send()
+            slot, copy = hand_over(i, blocks, pass_send, block_recv)
+            pl.when(jnp.logical_not(both(corner_mate, slot == 0)))(copy.wait_send)
 
     @pl.when(jnp.logical_not(jnp.logical_or(corner, sibling)))
     def _():
         for i in range(1, 4):
-            hand_over(i, halos, pass_halo, halo_recv)[1].wait_send()
+            slot, copy = hand_over(i, halos, pass_halo, halo_recv)
+            pl.when(jnp.logical_not(both(corner_mate, slot == 0)))(copy.wait_send)
 
     @pl.when(sibling)
     def _():
@@ -497,31 +503,21 @@
     second = jnp.where(far, MATES // 2, lax.rem(pj, 4))
     band = band_matrix()
 
-    def take(group, _):
+    def take(group, source):
         for half in range(2):
-            spread_halo(halos.at[group * 2 + half], margin, group, half)
-        outer_scale(table, margin, scale, group, band)
-        return 0
-
-    for g in range(4):
-        take(g, 0)
-
-    @pl.when(far)
-    def _():
-        take(4, 0)
+            spread_halo(halos.at[source * 2 + half], margin, group, half)
+        outer_scale(table, margin, scale, group, source, band)
 
     def write(group):
         return pltpu.make_async_copy(
             out.at[pl.ds(group * 8, 8)], result.at[pl.ds(group * 8, 8)], out_sem.at[group])
 
-    def step(group, _):
+    take(4, second)
+    for group in range(4):
+        take(group, group)
         for s in range(8):
-            outer_rows(group * 8, s, second, margin, scale, stage, inside, edge_stage.at[group * 8 + s], out, band)
+            outer_rows(group, s, margin, scale, stage, inside, edge_stage.at[group * 8 + s], out, band)
         write(group).start()
-        return 0
-
-    for g in range(4):
-        step(g, 0)
     for group in range(4):
         write(group).wait()
 
@@ -566,13 +562,14 @@
             pltpu.VMEM((2, 32, COLS), F32),
             pltpu.SemaphoreType.REGULAR,
             pltpu.SemaphoreType.REGULAR,
+            pltpu.SemaphoreType.REGULAR,
             pltpu.SemaphoreType.DMA,
             pltpu.SemaphoreType.DMA((2,)),
             pltpu.SemaphoreType.DMA((2,)),
-            pltpu.SemaphoreType.DMA((5,)),
+            pltpu.SemaphoreType.DMA((8,)),
             pltpu.SemaphoreType.DMA((MATES + 2,)),
             pltpu.SemaphoreType.DMA((7,)),
-            pltpu.SemaphoreType.DMA((5,)),
+            pltpu.SemaphoreType.DMA((8,)),
             pltpu.SemaphoreType.DMA((MATES + 2,)),
             pltpu.SemaphoreType.DMA((MATES,)),
             pltpu.SemaphoreType.DMA((4,)),

time: 18.8 us -> 18.4 us (0.979)
  Pallas kernels: 18.6 us -> 18.1 us
    pallas_call x1, Pallas kernels: 16.6 us -> 16.3 us  [per_device(): pl.pallas_call(gather_kernel, out_shape=(pltpu.VMEM((5 * 2 * STRIP * 8, C...]
    pallas_call x1, Pallas kernels: 2.04 us -> 1.77 us  [second_call(): pl.pallas_call(edge_kernel, out_shape=jax.ShapeDtypeStruct((32, 8, STRIP,...]
where the time goes in v5:
time: 18.4 us; the launch traced here: 18.1 us
  Pallas kernels  18.1 us (98%)
    pallas_call x1, Pallas kernels, per_device(): pl.pallas_call(gather_kernel, out_shape=(pltpu.VMEM((5 * 2 * STRIP * 8, C...  16.3 us
    pallas_call x1, Pallas kernels, second_call(): pl.pallas_call(edge_kernel, out_shape=jax.ShapeDtypeStruct((32, 8, STRIP,...  1.77 us

profile of v5, /device:TPU:238, one launch (start us, length us, event | category | flops | bytes accessed | tf_op | source)
XLA Modules:
  0.0 18.1 jit_solution(2079519430345154331)
XLA Ops:
  0.0 16.3 %coherence_inner.1 = (f32[1280,128]{1,0:T(8,128)S(1)}, bf16[10,48,128]{2,1,0:T(8,128)(2,1)S(1)}, f32[400,128]{1,0:T(8,128)S(1)}, f32[4096,128]{1,0:T(8,128)S(1)}, f32[3072,128]{1,0:T(8,128)S(1)}) custom-call(bf16[2,4,16,128]{3,2,1,0:T(8,128)(2,1)} %images.1), custom_call_target="tpu_custom_call" | custom-call | tf_op jit(solution)/shard_map/coherence_inner/pallas_call | solution.py:546
  16.3 1.8 %coherence_edges.1 = bf16[32,8,16,128]{3,2,1,0:T(8,128)(2,1)} custom-call(f32[1280,128]{1,0:T(8,128)S(1)} %get-tuple-element.10.table, bf16[10,48,128]{2,1,0:T(8,128)(2,1)S(1)} %get-tuple-element.11.halos, f32[400,128]{1,0:T(8,128)S(1)} %get-tuple-element.12.inner, f32[4096,128]{1,0:T(8,128)S(1)} %get-tuple-element.13.stage, ...), custom_call_target="tpu_custom_call" | custom-call | tf_op jit(solution)/shard_map/coherence_edges/pallas_call | solution.py:527

commit v6 on v5

--- a/solution.py
+++ b/solution.py
@@ -278,7 +278,7 @@
             src_ref=source, dst_ref=place.at[slot], send_sem=send_sem,
             recv_sem=recv_sem.at[slot], device_id=device, device_id_type=MESH)
 
-    sent, sent_by_corner = [], []
+    sent, sent_to_both = [], []
 
     def is_corner(device):
         return both(corner_mate, device["pj"] == 0)
@@ -288,7 +288,7 @@
         def _():
             copy.start()
 
-    def send_to_mates(source, place, send_sem, recv_sem):
+    def send_to_mates(source, place, send_sem, recv_sem, to_both_cores):
         for i, device in enumerate((mate(3), mate(2), mate(1), mate(0, 1))):
             target = jnp.where(both(is_corner(device), pj != 1), 1, device["pj"])
             copy = sending(source, place, pj, send_sem.at[1 + i], recv_sem, {"pj": target})
@@ -296,8 +296,8 @@
             sent.append(copy)
         for i in range(1, 4):
             copy = sending(source, place, pj, send_sem.at[4 + i], recv_sem, mate(i, 1))
-            send(copy, corner)
-            sent_by_corner.append(copy)
+            send(copy, to_both_cores)
+            sent_to_both.append((copy, to_both_cores))
 
     to_far = sending(own, blocks, MATES + core, block_send.at[0], block_recv, far_target)
     sent.append(to_far)
@@ -310,7 +310,7 @@
     def _():
         to_far.start()
 
-    send_to_mates(own, blocks, block_send, block_recv)
+    send_to_mates(own, blocks, block_send, block_recv, corner)
 
     @pl.when(corner)
     def _():
@@ -358,7 +358,7 @@
     far_halo = sending(halos.at[pj], halos, MATES + core, halo_send.at[0], halo_recv, far_target)
     far_halo.start()
     sent.append(far_halo)
-    send_to_mates(halos.at[pj], halos, halo_send, halo_recv)
+    send_to_mates(halos.at[pj], halos, halo_send, halo_recv, jnp.logical_or(corner, upper))
 
     def not_handed(slot):
         return jnp.logical_or(corner, both(corner_mate, slot == 0))
@@ -438,7 +438,11 @@
 
     pairs(0)
     pairs(1)
-    hand_all_over(halos, pass_halo, halo_recv)
+
+    @pl.when(jnp.logical_not(upper))
+    def _():
+        hand_all_over(halos, pass_halo, halo_recv)
+
     pairs(2)
 
     @pl.when(corner_mate)
@@ -450,7 +454,7 @@
     def halo_in(slot, _):
         @pl.when(slot != pj)
         def _():
-            @pl.when(jnp.logical_or(not_handed(slot), jnp.logical_or(lax.rem(slot, 2) != core, slot >= MATES)))
+            @pl.when(jnp.logical_or(jnp.logical_or(upper, not_handed(slot)), jnp.logical_or(lax.rem(slot, 2) != core, slot >= MATES)))
             def _():
                 arrived(slot, halos, halo_recv)
 
@@ -464,10 +468,8 @@
     for copy in sent:
         copy.wait_send()
 
-    @pl.when(corner)
-    def _():
-        for copy in sent_by_corner:
-            copy.wait_send()
+    for copy, condition in sent_to_both:
+        pl.when(condition)(copy.wait_send)
 
     @pl.when(jnp.logical_not(corner))
     def _():
@@ -475,7 +477,7 @@
             slot, copy = hand_over(i, blocks, pass_send, block_recv)
             pl.when(jnp.logical_not(both(corner_mate, slot == 0)))(copy.wait_send)
 
-    @pl.when(jnp.logical_not(jnp.logical_or(corner, sibling)))
+    @pl.when(jnp.logical_not(jnp.logical_or(upper, jnp.logical_or(corner, sibling))))
     def _():
         for i in range(1, 4):
             slot, copy = hand_over(i, halos, pass_halo, halo_recv)
@@ -508,18 +510,19 @@
             spread_halo(halos.at[source * 2 + half], margin, group, half)
         outer_scale(table, margin, scale, group, source, band)
 
-    def write(group):
+    def write(part):
         return pltpu.make_async_copy(
-            out.at[pl.ds(group * 8, 8)], result.at[pl.ds(group * 8, 8)], out_sem.at[group])
+            out.at[pl.ds(part * 4, 4)], result.at[pl.ds(part * 4, 4)], out_sem.at[part])
 
     take(4, second)
     for group in range(4):
         take(group, group)
         for s in range(8):
             outer_rows(group, s, margin, scale, stage, inside, edge_stage.at[group * 8 + s], out, band)
-        write(group).start()
-    for group in range(4):
-        write(group).wait()
+            if s % 4 == 3:
+                write(group * 2 + s // 4).start()
+    for part in range(8):
+        write(part).wait()
 
 
 def second_call(*kept):
@@ -534,7 +537,7 @@
             pltpu.VMEM((5 * 6 * 8, COLS), F32),
             pltpu.VMEM((32, 64, COLS), F32),
             pltpu.VMEM((32, 8, STRIP, COLS), BF),
-            pltpu.SemaphoreType.DMA((4,)),
+            pltpu.SemaphoreType.DMA((8,)),
         ],
         compiler_params=pltpu.CompilerParams(vmem_limit_bytes=16 << 20),
         name="coherence_edges",

time: 18.4 us -> 18.3 us (level)
  no operation moved by 1% of the time
where the time goes in v6:
time: 18.3 us; the launch traced here: 18.1 us
  Pallas kernels  18.1 us (99%)
    pallas_call x1, Pallas kernels, per_device(): pl.pallas_call(gather_kernel, out_shape=(pltpu.VMEM((5 * 2 * STRIP * 8, C...  16.3 us
    pallas_call x1, Pallas kernels, second_call(): pl.pallas_call(edge_kernel, out_shape=jax.ShapeDtypeStruct((32, 8, STRIP,...  1.76 us

profile of v6, /device:TPU:238, one launch (start us, length us, event | category | flops | bytes accessed | tf_op | source)
XLA Modules:
  0.0 18.1 jit_solution(2887633003091640083)
XLA Ops:
  0.0 16.3 %coherence_inner.1 = (f32[1280,128]{1,0:T(8,128)S(1)}, bf16[10,48,128]{2,1,0:T(8,128)(2,1)S(1)}, f32[400,128]{1,0:T(8,128)S(1)}, f32[4096,128]{1,0:T(8,128)S(1)}, f32[3072,128]{1,0:T(8,128)S(1)}) custom-call(bf16[2,4,16,128]{3,2,1,0:T(8,128)(2,1)} %images.1), custom_call_target="tpu_custom_call" | custom-call | tf_op jit(solution)/shard_map/coherence_inner/pallas_call | solution.py:549
  16.3 1.8 %coherence_edges.1 = bf16[32,8,16,128]{3,2,1,0:T(8,128)(2,1)} custom-call(f32[1280,128]{1,0:T(8,128)S(1)} %get-tuple-element.10.table, bf16[10,48,128]{2,1,0:T(8,128)(2,1)S(1)} %get-tuple-element.11.halos, f32[400,128]{1,0:T(8,128)S(1)} %get-tuple-element.12.inner, f32[4096,128]{1,0:T(8,128)S(1)} %get-tuple-element.13.stage, ...), custom_call_target="tpu_custom_call" | custom-call | tf_op jit(solution)/shard_map/coherence_edges/pallas_call | solution.py:530

commit v7 on v6

--- a/solution.py
+++ b/solution.py
@@ -535,7 +535,7 @@
         scratch_shapes=[
             pltpu.VMEM((5 * 2 * 6 * 8, COLS), F32),
             pltpu.VMEM((5 * 6 * 8, COLS), F32),
-            pltpu.VMEM((32, 64, COLS), F32),
+            pltpu.VMEM((32, 72, COLS), F32),
             pltpu.VMEM((32, 8, STRIP, COLS), BF),
             pltpu.SemaphoreType.DMA((8,)),
         ],
@@ -549,10 +549,10 @@
     kept = pl.pallas_call(
         gather_kernel,
         out_shape=(
-            pltpu.VMEM((5 * 2 * STRIP * 8, COLS), F32),
+            pltpu.VMEM((5 * 2 * STRIP * 8 + 64, COLS), F32),
             pltpu.VMEM((MATES + 2, 2 * EDGE, COLS), BF),
             pltpu.VMEM((5 * INNER * 8, COLS), F32),
-            pltpu.VMEM((32 * 8 * STRIP, COLS), F32),
+            pltpu.VMEM((32 * 8 * STRIP + 128, COLS), F32),
             pltpu.VMEM((32 * 12 * 8, COLS), F32),
         ),
         in_specs=[pl.BlockSpec(memory_space=pltpu.HBM)],

time: 18.3 us -> 18.3 us (level)
  no operation moved by 1% of the time
where the time goes in v7:
time: 18.3 us; the launch traced here: 18.1 us
  Pallas kernels  18.1 us (99%)
    pallas_call x1, Pallas kernels, per_device(): pl.pallas_call(gather_kernel, out_shape=(pltpu.VMEM((5 * 2 * STRIP * 8 +...  16.3 us
    pallas_call x1, Pallas kernels, second_call(): pl.pallas_call(edge_kernel, out_shape=jax.ShapeDtypeStruct((32, 8, STRIP,...  1.77 us

profile of v7, /device:TPU:238, one launch (start us, length us, event | category | flops | bytes accessed | tf_op | source)
XLA Modules:
  0.0 18.1 jit_solution(11847500107778494239)
XLA Ops:
  0.0 16.3 %coherence_inner.1 = (f32[1344,128]{1,0:T(8,128)S(1)}, bf16[10,48,128]{2,1,0:T(8,128)(2,1)S(1)}, f32[400,128]{1,0:T(8,128)S(1)}, f32[4224,128]{1,0:T(8,128)S(1)}, f32[3072,128]{1,0:T(8,128)S(1)}) custom-call(bf16[2,4,16,128]{3,2,1,0:T(8,128)(2,1)} %images.1), custom_call_target="tpu_custom_call" | custom-call | tf_op jit(solution)/shard_map/coherence_inner/pallas_call | solution.py:549
  16.3 1.8 %coherence_edges.1 = bf16[32,8,16,128]{3,2,1,0:T(8,128)(2,1)} custom-call(f32[1344,128]{1,0:T(8,128)S(1)} %get-tuple-element.10.table, bf16[10,48,128]{2,1,0:T(8,128)(2,1)S(1)} %get-tuple-element.11.halos, f32[400,128]{1,0:T(8,128)S(1)} %get-tuple-element.12.inner, f32[4224,128]{1,0:T(8,128)S(1)} %get-tuple-element.13.stage, ...), custom_call_target="tpu_custom_call" | custom-call | tf_op jit(solution)/shard_map/coherence_edges/pallas_call | solution.py:530
